TPU v7x, 256 devices: a whole 4x4x8 slice. The times are simulated.
256 devices in a mesh: fsdp: 8 (over z), expert: 32 (over y, x, core).
Axes of the slice: x: 4, y: 4, z: 8, core: 2. Of those that a mesh axis runs over, the one named last changes fastest.
Arguments:
- tokens: bfloat16 [12288, 4096], P(('fsdp', 'expert')), may hold values from -6 to 6
- expert_ids: int32 [12288, 8], P(('fsdp', 'expert')), may hold values from 0 to 31, all different within a row; in each aligned block of 48 rows (0 to 47, 48 to 95, ...) at most 18 rows name the same one
- gate_scale: float32 [12288, 8], P(('fsdp', 'expert')), may hold values from 0.05 to 0.5
- gate_up: bfloat16 [32, 4096, 1536], P('expert', 'fsdp'), may hold values from -0.09375 to 0.09375
- down: bfloat16 [32, 768, 4096], P('expert', 'fsdp'), may hold values from -0.21875 to 0.21875
Outputs:
- combined: bfloat16 [12288, 4096], P(('fsdp', 'expert'))
Inputs may be any that keep to these rules, and one draw needn't show every extreme that they name: `expert_ids`: each row names 8 different experts. Within each aligned block of 48 tokens (the rows of one device) no expert is named by more than 18 rows, and in every draw some expert is named by exactly 18 rows of some block.
All inputs are finite; a program needn't handle non-finite values.
Results may differ from a plain program's by a relative error of at most 0.0057.
Values may be sent and summed in bfloat16 or wider, within the bound.
No kernel may reach another device: no remote copies, remote signals or barrier semaphores. Data moves between devices by JAX's collectives and lax.ppermute only.
A program may use at most 128 MiB of HBM per device.

v0:
```python
import jax
import jax.numpy as jnp
from jax import lax
from jax.sharding import PartitionSpec as P

FF = 768
EXPERTS = 32
TOP = 8
CAP = 18


def body(tokens, expert_ids, gate_scale, gate_up, down):
    dest_count = lax.axis_size("expert")
    local_experts = EXPERTS // dest_count
    model_width = tokens.shape[1]
    tok_rows = tokens.shape[0]
    flat_ids = expert_ids.reshape(-1)
    onehot = (flat_ids[:, None] == jnp.arange(EXPERTS, dtype=jnp.int32)[None, :]).astype(jnp.int32)
    before = jnp.cumsum(onehot, axis=0) - onehot
    slot_index = jnp.sum(before * onehot, axis=1)
    places = flat_ids * CAP + slot_index
    slot_table = places.reshape(tok_rows, TOP)
    rows_all = jnp.arange(EXPERTS * CAP, dtype=jnp.int32)
    dispatch_matrix = jnp.any(rows_all[:, None, None] == slot_table[None, :, :], axis=2).astype(
        jnp.bfloat16
    )
    outgoing = jnp.dot(dispatch_matrix, tokens, preferred_element_type=jnp.float32).astype(
        jnp.bfloat16
    )
    outgoing = outgoing.reshape(dest_count, local_experts, CAP, model_width)
    incoming = lax.all_to_all(outgoing, "expert", split_axis=0, concat_axis=0, tiled=True)
    whole_in, whole_out = (
        lax.all_gather(gate_up, "fsdp", axis=1, tiled=True),
        lax.all_gather(down, "fsdp", axis=1, tiled=True),
    )
    both = jnp.einsum("sjcd,jdf->sjcf", incoming, whole_in, preferred_element_type=jnp.float32)
    hidden = (jax.nn.silu(both[..., :FF]) * both[..., FF:]).astype(jnp.bfloat16)
    result = jnp.einsum("sjch,jhd->sjcd", hidden, whole_out, preferred_element_type=jnp.float32)
    result = result.astype(jnp.bfloat16)
    returned = lax.all_to_all(result, "expert", split_axis=0, concat_axis=0, tiled=True)
    returned = returned.reshape(EXPERTS * CAP, model_width)
    picked = jnp.take(returned, places, axis=0).reshape(tok_rows, TOP, model_width)
    combined = jnp.sum(picked.astype(jnp.float32) * gate_scale[:, :, None], axis=1)
    return combined.astype(jnp.bfloat16)


def solution(mesh):
    return jax.shard_map(
        body,
        mesh=mesh,
        in_specs=(
            P(("fsdp", "expert"), None),
            P(("fsdp", "expert"), None),
            P(("fsdp", "expert"), None),
            P("expert", "fsdp", None),
            P("expert", "fsdp", None),
        ),
        out_specs=P(("fsdp", "expert"), None),
        check_vma=False,
    )
```

profile of v0, /device:TPU:64, one launch (start us, length us, event | category | flops | bytes accessed | tf_op | source)
XLA Modules:
  0.0 346.4 jit_solution(2029029037833623036)
XLA Ops:
  6.5 0.0 copy-start
  6.5 0.0 all-gather.3.cloned.1.call-start
  6.5 0.7 all-gather.3.cloned.1.call-update
  7.3 0.0 all-gather.5.cloned.1.call-start
  7.3 0.7 all-gather.5.cloned.1.call-update
  8.0 0.8 copy.33
  8.8 0.1 eq.39
  8.9 0.1 reshape.90
  9.0 0.9 reduce-window.6
  9.9 0.2 slice_reduce_fusion
  10.1 0.1 fusion.23
  10.2 0.1 reduce_sum.23
  10.3 0.1 copy.36
  10.4 0.7 compare_and_fusion
  11.1 0.1 copy.38
  11.2 0.4 fusion.18
  11.5 0.0 copy-done
  11.6 3.6 %convolution_convert_fusion = bf16[576,4096]{1,0:T(8,128)(2,1)} fusion(pred[576,48]{0,1:T(8,128)(4,1)S(1)} %fusion.18, bf16[48,4096]{1,0:T(8,128)(2,1)S(1)} %copy-done), kind=kOutput, calls=%fused_computation.7 | convolution fusion | flops 228851712 | bytes 5139456 | tf_op jit(solution)/shard_map/dot_general | solution.py:27
  15.2 7.6 %reshape.92 = bf16[32,1,18,4096]{3,2,0,1:T(8,128)(2,1)} reshape(bf16[576,4096]{1,0:T(8,128)(2,1)} %convolution_convert_fusion) | data formatting | bytes 9437184 | tf_op jit(solution)/shard_map/reshape | solution.py:30
  22.7 80.9 %all_to_all.10 = bf16[32,1,18,4096]{3,2,1,0:T(8,128)(2,1)} all-to-all(bf16[32,1,18,4096]{3,2,1,0:T(8,128)(2,1)} %bitcast.61), channel_id=1, replica_groups=mesh['fsdp'=8,'expert'=32] {'expert'}, dimensions={0} | all-to-all | bytes 9437184 | tf_op jit(solution)/shard_map/all_to_all | solution.py:31
  103.6 39.5 %all-gather.3.cloned.1.call-done = bf16[1,4096,1536]{2,1,0:T(8,128)(2,1)} async-done(((bf16[1,512,1536]{2,1,0:T(8,128)(2,1)}), bf16[1,4096,1536]{2,1,0:T(8,128)(2,1)}) %all-gather.3.cloned.1.call-update) | async-done | bytes 12582928 | tf_op jit(solution)/shard_map/all_gather | solution.py:33
  143.2 17.9 %fusion.12 = f32[32,1,18,1536]{3,0,2,1:T(8,128)} fusion(bf16[1,4096,1536]{2,1,0:T(8,128)(2,1)} %all-gather.3.cloned.1.call-done, bf16[32,1,18,4096]{3,2,1,0:T(8,128)(2,1)} %all_to_all.10), kind=kOutput, calls=%fused_computation.11 | convolution fusion | flops 7247757312 | bytes 20840448 | tf_op jit(solution)/shard_map/sjcd,jdf->sjcf/dot_general | solution.py:36
  161.0 57.0 %all-gather.5.cloned.1.call-done = bf16[1,768,4096]{2,1,0:T(8,128)(2,1)} async-done(((bf16[1,96,4096]{2,1,0:T(8,128)(2,1)}), bf16[1,768,4096]{2,1,0:T(8,128)(2,1)}) %all-gather.5.cloned.1.call-update) | async-done | bytes 6291472 | tf_op jit(solution)/shard_map/all_gather | solution.py:34
  218.1 7.7 %fusion.7 = bf16[32,1,18,4096]{3,0,2,1:T(8,128)(2,1)S(1)} fusion(bf16[1,768,4096]{2,1,0:T(8,128)(2,1)} %all-gather.5.cloned.1.call-done, f32[32,1,18,1536]{3,0,2,1:T(8,128)} %fusion.12), kind=kOutput, calls=%fused_computation.8 | convolution fusion | flops 3628892160 | bytes 14548992 | tf_op jit(solution)/shard_map/sjch,jhd->sjcd/dot_general | solution.py:38
  225.8 5.4 %copy.41 = bf16[32,1,18,4096]{3,2,1,0:T(8,128)(2,1)} copy(bf16[32,1,18,4096]{3,0,2,1:T(8,128)(2,1)S(1)} %fusion.7) | data formatting | bytes 9437184 | tf_op jit(solution)/shard_map/convert_element_type | solution.py:39
  231.2 0.0 copy-start.2
  231.2 0.0 copy-start.3
  231.2 7.6 %all-to-all-start.1 = ((bf16[32,1,18,4096]{3,2,1,0:T(8,128)(2,1)}), bf16[32,1,18,4096]{3,2,1,0:T(8,128)(2,1)}, u32[]{:S(2)}, u32[]{:S(2)}) async-start(bf16[32,1,18,4096]{3,2,1,0:T(8,128)(2,1)} %copy.41), calls=%async_computation.1 | async-start | bytes 12582912 | tf_op jit(solution)/shard_map/all_to_all | solution.py:40
  238.7 0.0 copy-done.2
  238.8 0.1 copy.42
  238.8 0.1 mul.44
  238.9 0.1 copy.37
  239.0 0.0 copy-done.3
  239.0 0.7 copy.43
  239.8 76.6 %all-to-all-done.1 = bf16[32,1,18,4096]{3,2,1,0:T(8,128)(2,1)} async-done(((bf16[32,1,18,4096]{3,2,1,0:T(8,128)(2,1)}), bf16[32,1,18,4096]{3,2,1,0:T(8,128)(2,1)}, u32[]{:S(2)}, u32[]{:S(2)}) %all-to-all-start.1) | async-done | bytes 4718624 | tf_op jit(solution)/shard_map/all_to_all | solution.py:40
  316.4 7.8 %reshape.97 = bf16[576,4096]{1,0:T(8,128)(2,1)} reshape(bf16[32,1,18,4096]{3,2,1,0:T(8,128)(2,1)} %all-to-all-done.1) | data formatting | bytes 9437184 | tf_op jit(solution)/shard_map/reshape | solution.py:41
  324.2 0.0 copy-start.1
  324.2 10.5 %gather_fusion = bf16[384,4096]{1,0:T(8,128)(2,1)S(1)} fusion(bf16[576,4096]{1,0:T(8,128)(2,1)} %reshape.97, s32[1024]{0:T(1024)S(1)} %pad_clamp_fusion), kind=kCustom, calls=%fused_computation | custom fusion | bytes 6292992 | tf_op jit(solution)/shard_map/jit(_take)/gather | solution.py:42
  334.7 4.8 %multiply_reduce_fusion = bf16[48,4096]{1,0:T(8,128)(2,1)} fusion(bf16[384,4096]{1,0:T(8,128)(2,1)S(1)} %gather_fusion, f32[48,8]{1,0:T(8,128)} %copy.43, pred[48,8]{1,0:T(8,128)(4,1)S(1)} %copy.37), kind=kLoop, calls=%fused_computation.5 | loop fusion | flops 6094848 | bytes 3540864 | tf_op jit(solution)/shard_map/reduce_sum | solution.py:43
  339.6 0.0 copy-done.1
  (5 shorter events, 0.1 us)
Async XLA Ops:
  6.5 5.0 %copy-start = (bf16[48,4096]{1,0:T(8,128)(2,1)S(1)}, bf16[48,4096]{1,0:T(8,128)(2,1)}, u32[]{:S(2)}) copy-start(bf16[48,4096]{1,0:T(8,128)(2,1)} %param.5) | copy-start | bytes 1179652
  6.5 136.6 %all-gather.3.cloned.1.call-start = ((), (), s32[]{:S(2)}) async-start(), calls=%async_computation.2 | async-start | bytes 14155776 | tf_op jit(solution)/shard_map/all_gather | solution.py:33
  7.3 210.8 %all-gather.5.cloned.1.call-start = ((), (), s32[]{:S(2)}) async-start(), calls=%async_computation.3 | async-start | bytes 7077888 | tf_op jit(solution)/shard_map/all_gather | solution.py:34
  231.2 7.6 %copy-start.2 = (s32[48,8]{0,1:T(8,128)S(1)}, s32[48,8]{0,1:T(8,128)}, u32[]{:S(2)}) copy-start(s32[48,8]{0,1:T(8,128)} %param.6) | copy-start | bytes 4612
  231.2 7.9 %copy-start.3 = (f32[48,8]{0,1:T(8,128)S(1)}, f32[48,8]{0,1:T(8,128)}, u32[]{:S(2)}) copy-start(f32[48,8]{0,1:T(8,128)} %param.7) | copy-start | bytes 4612
  231.2 85.2 %all-to-all-start.1 = ((bf16[32,1,18,4096]{3,2,1,0:T(8,128)(2,1)}), bf16[32,1,18,4096]{3,2,1,0:T(8,128)(2,1)}, u32[]{:S(2)}, u32[]{:S(2)}) async-start(bf16[32,1,18,4096]{3,2,1,0:T(8,128)(2,1)} %copy.41), calls=%async_computation.1 | async-start | bytes 12582912 | tf_op jit(solution)/shard_map/all_to_all | solution.py:40
  324.2 15.4 %copy-start.1 = (bf16[48,4096]{1,0:T(8,128)(2,1)S(1)}, bf16[48,4096]{1,0:T(8,128)(2,1)}, u32[]{:S(2)}) copy-start(bf16[48,4096]{1,0:T(8,128)(2,1)} %param.5) | copy-start | bytes 1179652
Sparse Core Ops, SparseCore 0:
  9.1 133.9 all-gather.2
  144.9 73.0 all-gather.4
where the time goes:
time: 348 us; the launch traced here: 346 us
  waiting for transfers between devices  175 us (50%)
  blocking collectives  80.9 us (23%)
  local copies, waits for them, and re-layouts  33.6 us (10%)
  matrix products  29.2 us (8%)
  between operations  13.5 us (4%)
  starting transfers between devices  7.6 us (2%)
  other arithmetic  6.98 us (2%)
    all_to_all x1, blocking collectives, body(): lax.all_to_all(outgoing, 'expert', split_axis=0, concat_axis=0, tiled=True)  80.9 us
    all_to_all x1, waiting for transfers between devices, body(): lax.all_to_all(result, 'expert', split_axis=0, concat_axis=0, tiled=True)  76.6 us
    all_gather x1, waiting for transfers between devices, body(): lax.all_gather(down, 'fsdp', axis=1, tiled=True)  57 us
    all_gather x1, waiting for transfers between devices, body(): lax.all_gather(gate_up, 'fsdp', axis=1, tiled=True)  39.5 us
    dot_general x1, matrix products, body(): jnp.einsum('sjcd,jdf->sjcf', incoming, whole_in, preferred_element_type=j...  17.9 us
    gather x1, local copies, waits for them, and re-layouts, body(): jnp.take(returned, places, axis=0).reshape(tok_rows, TOP, model_width)  10.5 us
    reshape x1, local copies, waits for them, and re-layouts, body(): returned = returned.reshape(EXPERTS * CAP, model_width)  7.79 us
    dot_general x1, matrix products, body(): jnp.einsum('sjch,jhd->sjcd', hidden, whole_out, preferred_element_type=jn...  7.72 us
  transfers between devices with their start and end apart: 3, of which 3 were waited for; matrix products, arithmetic and copies ran while one was open for 10% of the time, Pallas kernels for 0%

commit v1 on v0

v1 whole, which is shorter than its diff:
```python
import functools

import jax
import jax.numpy as jnp
from jax import lax
from jax.experimental import pallas as pl
from jax.experimental.pallas import tpu as pltpu
from jax.sharding import PartitionSpec as P

FF = 768
EXPERTS = 32
CAP = 18
MAIN = 16
SPILL = CAP - MAIN
LANES = 128
MIB = 1024 * 1024


def iota(shape, axis):
    return lax.broadcasted_iota(jnp.int32, shape, axis)


def dot(a, b):
    return jnp.dot(a, b, preferred_element_type=jnp.float32)


def as_bf16(mask):
    return mask.astype(jnp.float32).astype(jnp.bfloat16)


def spill_select():
    size = EXPERTS * MAIN
    row, col = iota((size, size), 0), iota((size, size), 1)
    return as_bf16(col == ((row & 63) >> 1) * MAIN + (row >> 6) * SPILL + (row & 1))


def dispatch_kernel(ids_ref, gates_ref, tokens_ref, out_ref, mix_ref, mix_spill_ref, select_ref):
    select_ref[...] = spill_select()
    rows, top = ids_ref.shape
    named = jnp.zeros((rows, EXPERTS), jnp.float32)
    gates = jnp.zeros((rows, EXPERTS), jnp.float32)
    for k in range(top):
        hit = ids_ref[:, k : k + 1] == iota((rows, EXPERTS), 1)
        named = named + hit.astype(jnp.float32)
        gates = gates + jnp.where(hit, gates_ref[:, k : k + 1], 0.0)
    named16 = named.astype(jnp.bfloat16)
    row, col = iota((rows, rows), 0), iota((rows, rows), 1)
    slots = dot(as_bf16(col < row), named16)
    over_tokens = (((0,), (0,)), ((), ()))
    named_t = lax.dot_general(named16, as_bf16(row == col), over_tokens, preferred_element_type=jnp.float32)
    slots_t = lax.dot_general(named16, as_bf16(row < col), over_tokens, preferred_element_type=jnp.float32)
    slots_t = jnp.where(named_t > 0.5, slots_t, -1.0)
    wide = jnp.broadcast_to(slots_t[:, None, :], (EXPERTS, MAIN, rows)).reshape(EXPERTS * MAIN, rows)
    place = iota((EXPERTS * MAIN, rows), 0) % MAIN
    pick = as_bf16(wide == place.astype(jnp.float32))
    width = tokens_ref.shape[1]
    blocks = width // LANES
    for b in range(0, blocks, 2):
        part = dot(pick, tokens_ref[:, b * LANES : (b + 2) * LANES]).astype(jnp.bfloat16)
        for i in range(2):
            out_ref[:, (b + i) * MAIN : (b + i + 1) * MAIN, :] = part[:, i * LANES : (i + 1) * LANES].reshape(
                EXPERTS, MAIN, LANES
            )
    picks = [
        as_bf16((place // SPILL == i) & (wide == (MAIN + place % SPILL).astype(jnp.float32))) for i in range(8)
    ]
    for g in range(blocks // 8):
        part = jnp.zeros((EXPERTS * MAIN, LANES), jnp.float32)
        for i in range(8):
            b = 8 * g + i
            part = part + dot(picks[i], tokens_ref[:, b * LANES : (b + 1) * LANES])
        start = blocks * MAIN + g * MAIN
        out_ref[:, start : start + MAIN, :] = part.astype(jnp.bfloat16).reshape(EXPERTS, MAIN, LANES)
    first = gates.astype(jnp.bfloat16)
    rest = gates - first.astype(jnp.float32)
    second = rest.astype(jnp.bfloat16)
    third = (rest - second.astype(jnp.float32)).astype(jnp.bfloat16)
    slots16 = slots.astype(jnp.bfloat16)
    for ref, per, base in ((mix_ref, MAIN, 0), (mix_spill_ref, SPILL, MAIN)):
        size = EXPERTS * per
        spread = as_bf16(iota((EXPERTS, size), 1) // per == iota((EXPERTS, size), 0))
        fits = dot(slots16, spread) == (base + iota((rows, size), 1) % per).astype(jnp.float32)
        for i, term in enumerate((first, second, third)):
            ref[i * rows : (i + 1) * rows, :] = jnp.where(fits, dot(term, spread), 0.0).astype(jnp.bfloat16)


def dispatch(ids, gates, tokens):
    rows, width = tokens.shape
    return pl.pallas_call(
        dispatch_kernel,
        out_shape=(
            jax.ShapeDtypeStruct((EXPERTS, CAP * width // LANES, LANES), jnp.bfloat16),
            jax.ShapeDtypeStruct((3 * rows, EXPERTS * MAIN), jnp.bfloat16),
            jax.ShapeDtypeStruct((3 * rows, EXPERTS * SPILL), jnp.bfloat16),
            jax.ShapeDtypeStruct((EXPERTS * MAIN, EXPERTS * MAIN), jnp.bfloat16),
        ),
        compiler_params=pltpu.CompilerParams(vmem_limit_bytes=60 * MIB),
    )(ids, gates, tokens)


def unpack_kernel(select_ref, in_ref, out_ref):
    width = out_ref.shape[1]
    blocks = width // LANES
    size = EXPERTS * MAIN
    for b in range(blocks):
        out_ref[:size, b * LANES : (b + 1) * LANES] = in_ref[:, b * MAIN : (b + 1) * MAIN, :].reshape(size, LANES)
    for g in range(blocks // 8):
        start = blocks * MAIN + g * MAIN
        part = dot(select_ref[...], in_ref[:, start : start + MAIN, :].reshape(size, LANES)).astype(jnp.bfloat16)
        for i in range(8):
            b = 8 * g + i
            out_ref[size:, b * LANES : (b + 1) * LANES] = part[i * 64 : (i + 1) * 64]


def unpack(select, incoming):
    width = incoming.shape[1] * LANES // CAP
    return pl.pallas_call(
        unpack_kernel,
        out_shape=jax.ShapeDtypeStruct((EXPERTS * CAP, width), jnp.bfloat16),
        compiler_params=pltpu.CompilerParams(vmem_limit_bytes=60 * MIB),
    )(select, incoming)


def gate_up_kernel(x_ref, gate_ref, up_ref, out_ref):
    gate = dot(x_ref[...], gate_ref[0])
    up = dot(x_ref[...], up_ref[0])
    out_ref[...] = (gate / (1.0 + jnp.exp(-gate)) * up).astype(jnp.bfloat16)


def gate_up_rows(x, weights, step=256):
    rows, width = x.shape
    steps = FF // step
    return pl.pallas_call(
        gate_up_kernel,
        grid=(steps,),
        in_specs=[
            pl.BlockSpec((rows, width), lambda j: (0, 0)),
            pl.BlockSpec((1, width, step), lambda j: (0, 0, j)),
            pl.BlockSpec((1, width, step), lambda j: (0, 0, steps + j)),
        ],
        out_specs=pl.BlockSpec((rows, step), lambda j: (0, j)),
        out_shape=jax.ShapeDtypeStruct((rows, FF), jnp.bfloat16),
        compiler_params=pltpu.CompilerParams(vmem_limit_bytes=60 * MIB),
    )(x, weights, weights)


def down_kernel(places_ref, select_ref, hidden_ref, *refs):
    pieces, (out_ref, held, sems) = refs[:-3], refs[-3:]
    depth = pieces[0].shape[1]
    copies = []
    for i, piece in enumerate(pieces):
        start = pl.multiple_of(places_ref[i] * depth, 32)
        copies.append(pltpu.make_async_copy(piece.at[0], held.at[pl.ds(start, depth), :], sems.at[i]))
        copies[-1].start()
    for copy in copies:
        copy.wait()
    blocks = held.shape[1] // LANES
    size = EXPERTS * MAIN
    for g in range(blocks // 8):
        spill = []
        for p in range(4):
            b = 8 * g + 2 * p
            weights = held[:, b * LANES : (b + 2) * LANES]
            part = dot(hidden_ref[...], weights).astype(jnp.bfloat16)
            for i in range(2):
                out_ref[:, (b + i) * MAIN : (b + i + 1) * MAIN, :] = part[
                    :size, i * LANES : (i + 1) * LANES
                ].reshape(EXPERTS, MAIN, LANES)
                spill.append(part[size:, i * LANES : (i + 1) * LANES])
        start = blocks * MAIN + g * MAIN
        out_ref[:, start : start + MAIN, :] = (
            lax.dot_general(
                select_ref[...],
                jnp.concatenate(spill, axis=0),
                (((0,), (0,)), ((), ())),
                preferred_element_type=jnp.float32,
            )
            .astype(jnp.bfloat16)
            .reshape(EXPERTS, MAIN, LANES)
        )


def down_rows(places, select, hidden, pieces):
    depth, width = pieces[0].shape[1:]
    count = len(pieces)
    return pl.pallas_call(
        down_kernel,
        in_specs=[pl.BlockSpec(memory_space=pltpu.SMEM)]
        + [pl.BlockSpec(memory_space=pltpu.VMEM)] * 2
        + [pl.BlockSpec(memory_space=pl.ANY)] * count,
        out_shape=jax.ShapeDtypeStruct((EXPERTS, CAP * width // LANES, LANES), jnp.bfloat16),
        scratch_shapes=[pltpu.VMEM((count * depth, width), jnp.bfloat16), pltpu.SemaphoreType.DMA((count,))],
        compiler_params=pltpu.CompilerParams(vmem_limit_bytes=60 * MIB),
    )(places, select, hidden, *pieces)


def combine_kernel(mix_ref, mix_spill_ref, select_ref, in_ref, *refs):
    out_ref = refs[-1]
    offset = 0
    if len(refs) == 2:
        offset = refs[0].shape[1]
        out_ref[:, :offset] = refs[0][...]
    blocks = in_ref.shape[1] // CAP
    size = EXPERTS * MAIN
    rows = out_ref.shape[0]
    for g in range(blocks // 8):
        start = blocks * MAIN + g * MAIN
        spill = dot(select_ref[...], in_ref[:, start : start + MAIN, :].reshape(size, LANES)).astype(jnp.bfloat16)
        for p in range(4):
            b = 8 * g + 2 * p
            main = jnp.concatenate(
                [in_ref[:, (b + i) * MAIN : (b + i + 1) * MAIN, :].reshape(size, LANES) for i in range(2)], axis=1
            )
            extra = jnp.concatenate([spill[(2 * p + i) * 64 : (2 * p + i + 1) * 64] for i in range(2)], axis=1)
            total = dot(mix_ref[...], main) + dot(mix_spill_ref[...], extra)
            total = total[2 * rows :] + total[rows : 2 * rows] + total[:rows]
            out_ref[:, offset + b * LANES : offset + (b + 2) * LANES] = total.astype(jnp.bfloat16)


def combine(mix, mix_spill, select, returned, *earlier):
    width = returned.shape[1] * LANES // CAP + sum([e.shape[1] for e in earlier])
    return pl.pallas_call(
        combine_kernel,
        out_shape=jax.ShapeDtypeStruct((mix.shape[0] // 3, width), jnp.bfloat16),
        compiler_params=pltpu.CompilerParams(vmem_limit_bytes=60 * MIB),
    )(mix, mix_spill, select, returned, *earlier)


STEPS = {1: 4, -1: 3}


def tie(value, others):
    return lax.optimization_barrier((value, tuple(others)))[0]


def body(tokens, expert_ids, gate_scale, gate_up, down):
    n, me = lax.axis_size("fsdp"), lax.axis_index("fsdp")
    split = down.shape[2] // 2
    weights = lax.all_gather(gate_up, "fsdp", axis=1, tiled=True)
    gathered = lax.all_gather(down[:, :, split:], "fsdp", axis=1, tiled=True)
    pieces, shards = [down[:, :, :split]], [me]
    latest = {way: pieces[0] for way in STEPS}
    for k in range(1, 5):
        for way, steps in STEPS.items():
            if k <= steps:
                latest[way] = lax.ppermute(latest[way], "fsdp", [(j, (j + way) % n) for j in range(n)])
                pieces.append(latest[way])
                shards.append((me - way * k + n) % n)
    places = jnp.stack(shards).astype(jnp.int32)

    outgoing, mix, mix_spill, select = dispatch(expert_ids, gate_scale, tokens)
    incoming = lax.all_to_all(outgoing, "expert", split_axis=0, concat_axis=0, tiled=True)
    x = unpack(select, incoming)
    hidden = gate_up_rows(tie(x, pieces[1:]), weights)

    result = []
    for places, pieces in ((places, pieces), (jnp.zeros((1,), jnp.int32), [gathered])):
        rows = down_rows(places, select, hidden, pieces)
        returned = lax.all_to_all(rows, "expert", split_axis=0, concat_axis=0, tiled=True)
        result = [combine(mix, mix_spill, select, returned, *result)]
    return result[0]


def solution(mesh):
    return jax.shard_map(
        body,
        mesh=mesh,
        in_specs=(
            P(("fsdp", "expert"), None),
            P(("fsdp", "expert"), None),
            P(("fsdp", "expert"), None),
            P("expert", "fsdp", None),
            P("expert", "fsdp", None),
        ),
        out_specs=P(("fsdp", "expert"), None),
        check_vma=False,
    )
```

time: 348 us -> 287 us (0.82)
  blocking collectives: 80.9 us -> 0 us
  Pallas kernels: 0 us -> 47.6 us
  local copies, waits for them, and re-layouts: 33.6 us -> 4.22 us
  matrix products: 29.2 us -> 0 us
  starting transfers between devices: 7.6 us -> 31.6 us
  waiting for transfers between devices: 175 us -> 187 us
  other arithmetic: 6.98 us -> 0 us
    all_to_all x1 -> x0, blocking collectives: 80.9 us -> none  [body(): lax.all_to_all(outgoing, 'expert', split_axis=0, concat_axis=0, tiled=True)]
    ppermute x0 -> x7, waiting for transfers between devices: none -> 62.3 us  [body(): lax.ppermute(latest[way], 'fsdp', [(j, (j + way) % n) for j in range(n)])]
    pallas_call x0 -> x7, Pallas kernels: none -> 47.6 us  [the longest x2 14.6 us: down_rows(): pl.pallas_call(down_kernel, in_specs=[pl.BlockSpec(memory_space=pltpu.SME...]
    all_to_all x1 -> x3, waiting for transfers between devices: 76.6 us -> 34.1 us  [the longest x2 34.1 us: body(): lax.all_to_all(rows, 'expert', split_axis=0, concat_axis=0, tiled=True)]
    dot_general x3 -> x0, matrix products: 29.2 us -> none  [the longest x1 17.9 us: body(): jnp.einsum('sjcd,jdf->sjcf', incoming, whole_in, preferred_element_type=j...]
    reshape x3 -> x0, local copies, waits for them, and re-layouts: 15.4 us -> none  [the longest x1 7.79 us: body(): returned = returned.reshape(EXPERTS * CAP, model_width)]
    ppermute x0 -> x7, starting transfers between devices: none -> 12.1 us  [body(): lax.ppermute(latest[way], 'fsdp', [(j, (j + way) % n) for j in range(n)])]
    all_to_all x1 -> x3, starting transfers between devices: 7.56 us -> 19.5 us  [the longest x2 11.9 us: body(): lax.all_to_all(rows, 'expert', split_axis=0, concat_axis=0, tiled=True)]
  transfers between devices with their start and end apart: 3 -> 12, of which waited for: 3 -> 10; matrix products, arithmetic and copies ran while one was open for 10% -> 1% of each run, Pallas kernels for 0% -> 15%
where the time goes in v1:
time: 287 us; the launch traced here: 284 us
  waiting for transfers between devices  187 us (65%)
  Pallas kernels  47.6 us (17%)
  starting transfers between devices  31.6 us (11%)
  between operations  13.5 us (5%)
  local copies, waits for them, and re-layouts  4.22 us (1%)
    all_gather x1, waiting for transfers between devices, body(): weights = lax.all_gather(gate_up, 'fsdp', axis=1, tiled=True)  69.5 us
    ppermute x7, waiting for transfers between devices, body(): lax.ppermute(latest[way], 'fsdp', [(j, (j + way) % n) for j in range(n)])  62.3 us
    all_to_all x2, waiting for transfers between devices, body(): lax.all_to_all(rows, 'expert', split_axis=0, concat_axis=0, tiled=True)  34.1 us
    all_gather x1, waiting for transfers between devices, body(): gathered = lax.all_gather(down[:, :, split:], 'fsdp', axis=1, tiled=True)  20.8 us
    pallas_call x2, Pallas kernels, down_rows(): pl.pallas_call(down_kernel, in_specs=[pl.BlockSpec(memory_space=pltpu.SME...  14.6 us
    pallas_call x1, Pallas kernels, gate_up_rows(): pl.pallas_call(gate_up_kernel, grid=(steps,), in_specs=[pl.BlockSpec((row...  12.3 us
    ppermute x7, starting transfers between devices, body(): lax.ppermute(latest[way], 'fsdp', [(j, (j + way) % n) for j in range(n)])  12.1 us
    all_to_all x2, starting transfers between devices, body(): lax.all_to_all(rows, 'expert', split_axis=0, concat_axis=0, tiled=True)  11.9 us
  transfers between devices with their start and end apart: 12, of which 10 were waited for; matrix products, arithmetic and copies ran while one was open for 1% of the time, Pallas kernels for 15%

profile of v1, /device:TPU:64, one launch (start us, length us, event | category | flops | bytes accessed | tf_op | source)
XLA Modules:
  0.0 284.3 jit_solution(14204407654658089338)
XLA Ops:
  6.5 0.0 all-gather.3.cloned.1.call-start
  6.5 0.7 all-gather.3.cloned.1.call-update
  7.3 1.4 copy.6.ids_ref
  8.6 1.4 copy.7.gates_ref
  10.0 6.2 %shard_map.55 = (bf16[32,576,128]{2,1,0:T(8,128)(2,1)}, bf16[144,512]{1,0:T(8,128)(2,1)}, bf16[144,64]{1,0:T(8,128)(2,1)}, bf16[512,512]{1,0:T(8,128)(2,1)}) custom-call(s32[48,8]{1,0:T(8,128)} %copy.6.ids_ref, f32[48,8]{1,0:T(8,128)} %copy.7.gates_ref, bf16[48,4096]{1,0:T(8,128)(2,1)} %tokens_ref.1), custom_call_target="tpu_custom_call" | custom-call | tf_op jit(solution)/shard_map/pallas_call | solution.py:89
  16.2 0.0 copy-start.2
  16.2 7.6 %all-to-all-start = ((bf16[32,576,128]{2,1,0:T(8,128)(2,1)}), bf16[32,576,128]{2,1,0:T(8,128)(2,1)}, u32[]{:S(2)}, u32[]{:S(2)}) async-start(bf16[32,576,128]{2,1,0:T(8,128)(2,1)} %get-tuple-element.13), calls=%async_computation | async-start | bytes 9437184 | tf_op jit(solution)/shard_map/all_to_all | solution.py:252
  23.8 0.0 all-gather.5.cloned.1.call-start
  23.9 0.0 copy-done.2
  23.9 0.8 fusion
  24.7 0.0 copy-start.1
  24.7 0.0 all-gather.5.cloned.1.call-update
  24.7 2.0 collective-permute-start
  26.7 0.1 collective-permute-start.1
  26.8 18.1 %collective-permute-done.refs_1_ = bf16[1,96,2048]{2,1,0:T(8,128)(2,1)S(1)} collective-permute-done((bf16[1,96,2048]{2,1,0:T(8,128)(2,1)S(1)}, bf16[1,96,2048]{2,1,0:T(8,128)(2,1)S(1)}, u32[]{:S(2)}, u32[]{:S(2)}) %collective-permute-start) | collective-permute-done | bytes 393248 | tf_op jit(solution)/shard_map/ppermute | solution.py:246
  44.9 0.0 copy-start.3
  44.9 2.6 collective-permute-start.2
  47.5 0.5 collective-permute-done.1.refs_2_
  47.9 0.0 copy-start.4
  47.9 0.0 collective-permute-start.3
  47.9 16.9 %collective-permute-done.2.refs_3_ = bf16[1,96,2048]{2,1,0:T(8,128)(2,1)S(1)} collective-permute-done((bf16[1,96,2048]{2,1,0:T(8,128)(2,1)S(1)}, bf16[1,96,2048]{2,1,0:T(8,128)(2,1)S(1)}, u32[]{:S(2)}, u32[]{:S(2)}) %collective-permute-start.2) | collective-permute-done | bytes 393248 | tf_op jit(solution)/shard_map/ppermute | solution.py:246
  64.8 0.0 copy-start.5
  64.8 3.7 %collective-permute-start.4 = (bf16[1,96,2048]{2,1,0:T(8,128)(2,1)S(1)}, bf16[1,96,2048]{2,1,0:T(8,128)(2,1)S(1)}, u32[]{:S(2)}, u32[]{:S(2)}) collective-permute-start(bf16[1,96,2048]{2,1,0:T(8,128)(2,1)S(1)} %collective-permute-done.2.refs_3_), channel_id=1, source_target_pairs={{0,32},{32,64},{64,96},{96,128},{128,160},{160,192},{192,224},{224... | collective-permute-start | bytes 1179656 | tf_op jit(solution)/shard_map/ppermute | solution.py:246
  68.6 0.5 collective-permute-done.3.refs_4_
  69.0 0.0 copy-start.6
  69.0 0.0 collective-permute-start.5
  69.0 16.7 %collective-permute-done.4.refs_5_ = bf16[1,96,2048]{2,1,0:T(8,128)(2,1)S(1)} collective-permute-done((bf16[1,96,2048]{2,1,0:T(8,128)(2,1)S(1)}, bf16[1,96,2048]{2,1,0:T(8,128)(2,1)S(1)}, u32[]{:S(2)}, u32[]{:S(2)}) %collective-permute-start.4) | collective-permute-done | bytes 393248 | tf_op jit(solution)/shard_map/ppermute | solution.py:246
  85.7 0.0 copy-start.7
  85.7 3.7 %collective-permute-start.6 = (bf16[1,96,2048]{2,1,0:T(8,128)(2,1)S(1)}, bf16[1,96,2048]{2,1,0:T(8,128)(2,1)S(1)}, u32[]{:S(2)}, u32[]{:S(2)}) collective-permute-start(bf16[1,96,2048]{2,1,0:T(8,128)(2,1)S(1)} %collective-permute-done.4.refs_5_), channel_id=1, source_target_pairs={{0,32},{32,64},{64,96},{96,128},{128,160},{160,192},{192,224},{224... | collective-permute-start | bytes 1179656 | tf_op jit(solution)/shard_map/ppermute | solution.py:246
  89.4 0.6 stack.35.places_ref
  90.0 0.0 all-to-all-done.in_ref
  90.0 6.4 %shard_map.56.x_ref = bf16[576,4096]{1,0:T(8,128)(2,1)} custom-call(bf16[512,512]{1,0:T(8,128)(2,1)} %get-tuple-element.12.select_ref, bf16[32,576,128]{2,1,0:T(8,128)(2,1)} %all-to-all-done.in_ref), custom_call_target="tpu_custom_call" | custom-call | tf_op jit(solution)/shard_map/pallas_call | solution.py:117
  96.5 0.0 copy-done.1
  96.5 0.0 copy-done.3
  96.5 0.0 copy-done.4
  96.5 0.0 copy-done.5
  96.5 0.0 copy-done.6
  96.5 0.0 copy-done.7
  96.5 0.0 collective-permute-done.5.refs_6_
  96.5 0.0 copy-start.8
  96.5 9.7 %collective-permute-done.6.refs_7_ = bf16[1,96,2048]{2,1,0:T(8,128)(2,1)S(1)} collective-permute-done((bf16[1,96,2048]{2,1,0:T(8,128)(2,1)S(1)}, bf16[1,96,2048]{2,1,0:T(8,128)(2,1)S(1)}, u32[]{:S(2)}, u32[]{:S(2)}) %collective-permute-start.6) | collective-permute-done | bytes 393248 | tf_op jit(solution)/shard_map/ppermute | solution.py:246
  106.3 0.0 copy-start.9
  106.3 69.5 %all-gather.3.cloned.1.call-done.gate_ref.up_ref = bf16[1,4096,1536]{2,1,0:T(8,128)(2,1)} async-done(((bf16[1,512,1536]{2,1,0:T(8,128)(2,1)}), bf16[1,4096,1536]{2,1,0:T(8,128)(2,1)}) %all-gather.3.cloned.1.call-update) | async-done | bytes 12582928 | tf_op jit(solution)/shard_map/all_gather | solution.py:239
  175.8 12.3 %shard_map.57.hidden_ref = bf16[576,768]{1,0:T(8,128)(2,1)} custom-call(bf16[576,4096]{1,0:T(8,128)(2,1)} %shard_map.56.x_ref, bf16[1,4096,1536]{2,1,0:T(8,128)(2,1)} %all-gather.3.cloned.1.call-done.gate_ref.up_ref, bf16[1,4096,1536]{2,1,0:T(8,128)(2,1)} %all-gather.3.cloned.1.call-done.gate_ref.up_ref), custom_call_target="tpu_custom_call" | custom-call | tf_op jit(solution)/shard_map/pallas_call | solution.py:133
  188.1 0.0 copy-done.8
  188.1 0.0 copy-done.9
  188.1 7.3 %shard_map.59 = bf16[32,288,128]{2,1,0:T(8,128)(2,1)} custom-call(s32[8]{0:T(128)} %stack.35.places_ref, bf16[512,512]{1,0:T(8,128)(2,1)} %get-tuple-element.12.select_ref, bf16[576,768]{1,0:T(8,128)(2,1)} %shard_map.57.hidden_ref, bf16[1,96,2048]{2,1,0:T(8,128)(2,1)} %copy-done.1, bf16[1,96,2048]{2,1,0:T(8,128)(2,1)} %copy-done.3, ...), custom_call_target="tpu_custom_call" | custom-call | tf_op jit(solution)/shard_map/pallas_call | solution.py:186
  195.4 7.1 %all-to-all-start.2 = ((bf16[32,288,128]{2,1,0:T(8,128)(2,1)}), bf16[32,288,128]{2,1,0:T(8,128)(2,1)S(1)}, u32[]{:S(2)}, u32[]{:S(2)}) async-start(bf16[32,288,128]{2,1,0:T(8,128)(2,1)} %shard_map.59), calls=%async_computation.2 | async-start | bytes 4718592 | tf_op jit(solution)/shard_map/all_to_all | solution.py:259
  202.5 20.8 %all-gather.5.cloned.1.call-done.refs_0_ = bf16[1,768,2048]{2,1,0:T(8,128)(2,1)} async-done(((bf16[1,96,2048]{2,1,0:T(8,128)(2,1)}), bf16[1,768,2048]{2,1,0:T(8,128)(2,1)}) %all-gather.5.cloned.1.call-update) | async-done | bytes 3145744 | tf_op jit(solution)/shard_map/all_gather | solution.py:240
  223.3 7.2 %shard_map.58 = bf16[32,288,128]{2,1,0:T(8,128)(2,1)} custom-call(s32[1]{0:T(128)} %constant.60.clone.1.places_ref, bf16[512,512]{1,0:T(8,128)(2,1)} %get-tuple-element.12.select_ref, bf16[576,768]{1,0:T(8,128)(2,1)} %shard_map.57.hidden_ref, bf16[1,768,2048]{2,1,0:T(8,128)(2,1)} %all-gather.5.cloned.1.call-done.refs_0_), custom_call_target="tpu_custom_call" | custom-call | tf_op jit(solution)/shard_map/pallas_call | solution.py:186
  230.6 5.0 %all-to-all-done.2.in_ref = bf16[32,288,128]{2,1,0:T(8,128)(2,1)S(1)} async-done(((bf16[32,288,128]{2,1,0:T(8,128)(2,1)}), bf16[32,288,128]{2,1,0:T(8,128)(2,1)S(1)}, u32[]{:S(2)}, u32[]{:S(2)}) %all-to-all-start.2) | async-done | bytes 2359328 | tf_op jit(solution)/shard_map/all_to_all | solution.py:259
  235.6 0.0 copy-start
  235.6 4.8 %all-to-all-start.1 = ((bf16[32,288,128]{2,1,0:T(8,128)(2,1)}), bf16[32,288,128]{2,1,0:T(8,128)(2,1)}, u32[]{:S(2)}, u32[]{:S(2)}) async-start(bf16[32,288,128]{2,1,0:T(8,128)(2,1)} %shard_map.58), calls=%async_computation.1 | async-start | bytes 4718592 | tf_op jit(solution)/shard_map/all_to_all | solution.py:259
  240.4 0.0 copy-done
  240.4 4.0 %shard_map.60.refs_0_ = bf16[48,2048]{1,0:T(8,128)(2,1)} custom-call(bf16[144,512]{1,0:T(8,128)(2,1)} %get-tuple-element.10.mix_ref, bf16[144,64]{1,0:T(8,128)(2,1)} %get-tuple-element.11.mix_spill_ref, bf16[512,512]{1,0:T(8,128)(2,1)} %get-tuple-element.12.select_ref, bf16[32,288,128]{2,1,0:T(8,128)(2,1)} %copy-done), custom_call_target="tpu_custom_call" | custom-call | tf_op jit(solution)/shard_map/pallas_call | solution.py:222
  244.4 29.1 %all-to-all-done.1.in_ref = bf16[32,288,128]{2,1,0:T(8,128)(2,1)} async-done(((bf16[32,288,128]{2,1,0:T(8,128)(2,1)}), bf16[32,288,128]{2,1,0:T(8,128)(2,1)}, u32[]{:S(2)}, u32[]{:S(2)}) %all-to-all-start.1) | async-done | bytes 2359328 | tf_op jit(solution)/shard_map/all_to_all | solution.py:259
  273.5 4.0 %shard_map.61 = bf16[48,4096]{1,0:T(8,128)(2,1)} custom-call(bf16[144,512]{1,0:T(8,128)(2,1)} %get-tuple-element.10.mix_ref, bf16[144,64]{1,0:T(8,128)(2,1)} %get-tuple-element.11.mix_spill_ref, bf16[512,512]{1,0:T(8,128)(2,1)} %get-tuple-element.12.select_ref, bf16[32,288,128]{2,1,0:T(8,128)(2,1)} %all-to-all-done.1.in_ref, bf16[48,2048]{1,0:T(8,128)(2,1)} %shard_map.60.refs_0_), custom_call_target="tpu_custom_call" | custom-call | tf_op jit(solution)/shard_map/pallas_call | solution.py:222
Async XLA Ops:
  6.5 169.2 %all-gather.3.cloned.1.call-start = ((), (), s32[]{:S(2)}) async-start(), calls=%async_computation.3 | async-start | bytes 14155776 | tf_op jit(solution)/shard_map/all_gather | solution.py:239
  16.2 7.6 %copy-start.2 = (bf16[1,96,4096]{2,1,0:T(8,128)(2,1)S(1)}, bf16[1,96,4096]{2,1,0:T(8,128)(2,1)}, u32[]{:S(2)}) copy-start(bf16[1,96,4096]{2,1,0:T(8,128)(2,1)} %param.9) | copy-start | bytes 2359300
  16.2 73.8 %all-to-all-start = ((bf16[32,576,128]{2,1,0:T(8,128)(2,1)}), bf16[32,576,128]{2,1,0:T(8,128)(2,1)}, u32[]{:S(2)}, u32[]{:S(2)}) async-start(bf16[32,576,128]{2,1,0:T(8,128)(2,1)} %get-tuple-element.13), calls=%async_computation | async-start | bytes 9437184 | tf_op jit(solution)/shard_map/all_to_all | solution.py:252
  23.8 199.5 %all-gather.5.cloned.1.call-start = ((), (), s32[]{:S(2)}) async-start(), calls=%async_computation.4 | async-start | bytes 3538944 | tf_op jit(solution)/shard_map/all_gather | solution.py:240
  24.7 71.8 %copy-start.1 = (bf16[1,96,2048]{2,1,0:T(8,128)(2,1)}, bf16[1,96,2048]{2,1,0:T(8,128)(2,1)S(1)}, u32[]{:S(2)}) copy-start(bf16[1,96,2048]{2,1,0:T(8,128)(2,1)S(1)} %get-tuple-element.16.refs_0_) | copy-start | bytes 1179652
  24.7 20.2 %collective-permute-start = (bf16[1,96,2048]{2,1,0:T(8,128)(2,1)S(1)}, bf16[1,96,2048]{2,1,0:T(8,128)(2,1)S(1)}, u32[]{:S(2)}, u32[]{:S(2)}) collective-permute-start(bf16[1,96,2048]{2,1,0:T(8,128)(2,1)S(1)} %get-tuple-element.16.refs_0_), channel_id=1, source_target_pairs={{0,32},{32,64},{64,96},{96,128},{128,160},{160,192},{192,224},{224... | collective-permute-start | bytes 1179656 | tf_op jit(solution)/shard_map/ppermute | solution.py:246
  26.7 21.2 %collective-permute-start.1 = (bf16[1,96,2048]{2,1,0:T(8,128)(2,1)S(1)}, bf16[1,96,2048]{2,1,0:T(8,128)(2,1)S(1)}, u32[]{:S(2)}, u32[]{:S(2)}) collective-permute-start(bf16[1,96,2048]{2,1,0:T(8,128)(2,1)S(1)} %get-tuple-element.16.refs_0_), channel_id=1, source_target_pairs={{0,224},{32,0},{64,32},{96,64},{128,96},{160,128},{192,160},{224,1... | collective-permute-start | bytes 1179656 | tf_op jit(solution)/shard_map/ppermute | solution.py:246
  44.9 51.6 %copy-start.3 = (bf16[1,96,2048]{2,1,0:T(8,128)(2,1)}, bf16[1,96,2048]{2,1,0:T(8,128)(2,1)S(1)}, u32[]{:S(2)}) copy-start(bf16[1,96,2048]{2,1,0:T(8,128)(2,1)S(1)} %collective-permute-done.refs_1_) | copy-start | bytes 1179652
  44.9 19.9 %collective-permute-start.2 = (bf16[1,96,2048]{2,1,0:T(8,128)(2,1)S(1)}, bf16[1,96,2048]{2,1,0:T(8,128)(2,1)S(1)}, u32[]{:S(2)}, u32[]{:S(2)}) collective-permute-start(bf16[1,96,2048]{2,1,0:T(8,128)(2,1)S(1)} %collective-permute-done.refs_1_), channel_id=1, source_target_pairs={{0,32},{32,64},{64,96},{96,128},{128,160},{160,192},{192,224},{224... | collective-permute-start | bytes 1179656 | tf_op jit(solution)/shard_map/ppermute | solution.py:246
  47.9 48.6 %copy-start.4 = (bf16[1,96,2048]{2,1,0:T(8,128)(2,1)}, bf16[1,96,2048]{2,1,0:T(8,128)(2,1)S(1)}, u32[]{:S(2)}) copy-start(bf16[1,96,2048]{2,1,0:T(8,128)(2,1)S(1)} %collective-permute-done.1.refs_2_) | copy-start | bytes 1179652
  47.9 21.1 %collective-permute-start.3 = (bf16[1,96,2048]{2,1,0:T(8,128)(2,1)S(1)}, bf16[1,96,2048]{2,1,0:T(8,128)(2,1)S(1)}, u32[]{:S(2)}, u32[]{:S(2)}) collective-permute-start(bf16[1,96,2048]{2,1,0:T(8,128)(2,1)S(1)} %collective-permute-done.1.refs_2_), channel_id=1, source_target_pairs={{0,224},{32,0},{64,32},{96,64},{128,96},{160,128},{192,160},{224,1... | collective-permute-start | bytes 1179656 | tf_op jit(solution)/shard_map/ppermute | solution.py:246
  64.8 31.6 %copy-start.5 = (bf16[1,96,2048]{2,1,0:T(8,128)(2,1)}, bf16[1,96,2048]{2,1,0:T(8,128)(2,1)S(1)}, u32[]{:S(2)}) copy-start(bf16[1,96,2048]{2,1,0:T(8,128)(2,1)S(1)} %collective-permute-done.2.refs_3_) | copy-start | bytes 1179652
  64.8 20.8 %collective-permute-start.4 = (bf16[1,96,2048]{2,1,0:T(8,128)(2,1)S(1)}, bf16[1,96,2048]{2,1,0:T(8,128)(2,1)S(1)}, u32[]{:S(2)}, u32[]{:S(2)}) collective-permute-start(bf16[1,96,2048]{2,1,0:T(8,128)(2,1)S(1)} %collective-permute-done.2.refs_3_), channel_id=1, source_target_pairs={{0,32},{32,64},{64,96},{96,128},{128,160},{160,192},{192,224},{224... | collective-permute-start | bytes 1179656 | tf_op jit(solution)/shard_map/ppermute | solution.py:246
  69.0 27.5 %copy-start.6 = (bf16[1,96,2048]{2,1,0:T(8,128)(2,1)}, bf16[1,96,2048]{2,1,0:T(8,128)(2,1)S(1)}, u32[]{:S(2)}) copy-start(bf16[1,96,2048]{2,1,0:T(8,128)(2,1)S(1)} %collective-permute-done.3.refs_4_) | copy-start | bytes 1179652
  69.0 27.5 %collective-permute-start.5 = (bf16[1,96,2048]{2,1,0:T(8,128)(2,1)S(1)}, bf16[1,96,2048]{2,1,0:T(8,128)(2,1)S(1)}, u32[]{:S(2)}, u32[]{:S(2)}) collective-permute-start(bf16[1,96,2048]{2,1,0:T(8,128)(2,1)S(1)} %collective-permute-done.3.refs_4_), channel_id=1, source_target_pairs={{0,224},{32,0},{64,32},{96,64},{128,96},{160,128},{192,160},{224,1... | collective-permute-start | bytes 1179656 | tf_op jit(solution)/shard_map/ppermute | solution.py:246
  85.7 10.8 %copy-start.7 = (bf16[1,96,2048]{2,1,0:T(8,128)(2,1)}, bf16[1,96,2048]{2,1,0:T(8,128)(2,1)S(1)}, u32[]{:S(2)}) copy-start(bf16[1,96,2048]{2,1,0:T(8,128)(2,1)S(1)} %collective-permute-done.4.refs_5_) | copy-start | bytes 1179652
  85.7 20.6 %collective-permute-start.6 = (bf16[1,96,2048]{2,1,0:T(8,128)(2,1)S(1)}, bf16[1,96,2048]{2,1,0:T(8,128)(2,1)S(1)}, u32[]{:S(2)}, u32[]{:S(2)}) collective-permute-start(bf16[1,96,2048]{2,1,0:T(8,128)(2,1)S(1)} %collective-permute-done.4.refs_5_), channel_id=1, source_target_pairs={{0,32},{32,64},{64,96},{96,128},{128,160},{160,192},{192,224},{224... | collective-permute-start | bytes 1179656 | tf_op jit(solution)/shard_map/ppermute | solution.py:246
  96.5 91.5 %copy-start.8 = (bf16[1,96,2048]{2,1,0:T(8,128)(2,1)}, bf16[1,96,2048]{2,1,0:T(8,128)(2,1)S(1)}, u32[]{:S(2)}) copy-start(bf16[1,96,2048]{2,1,0:T(8,128)(2,1)S(1)} %collective-permute-done.5.refs_6_) | copy-start | bytes 1179652
  106.3 81.8 %copy-start.9 = (bf16[1,96,2048]{2,1,0:T(8,128)(2,1)}, bf16[1,96,2048]{2,1,0:T(8,128)(2,1)S(1)}, u32[]{:S(2)}) copy-start(bf16[1,96,2048]{2,1,0:T(8,128)(2,1)S(1)} %collective-permute-done.6.refs_7_) | copy-start | bytes 1179652
  195.4 40.2 %all-to-all-start.2 = ((bf16[32,288,128]{2,1,0:T(8,128)(2,1)}), bf16[32,288,128]{2,1,0:T(8,128)(2,1)S(1)}, u32[]{:S(2)}, u32[]{:S(2)}) async-start(bf16[32,288,128]{2,1,0:T(8,128)(2,1)} %shard_map.59), calls=%async_computation.2 | async-start | bytes 4718592 | tf_op jit(solution)/shard_map/all_to_all | solution.py:259
  235.6 4.8 %copy-start = (bf16[32,288,128]{2,1,0:T(8,128)(2,1)}, bf16[32,288,128]{2,1,0:T(8,128)(2,1)S(1)}, u32[]{:S(2)}) copy-start(bf16[32,288,128]{2,1,0:T(8,128)(2,1)S(1)} %all-to-all-done.2.in_ref) | copy-start | bytes 7077892
  235.6 37.9 %all-to-all-start.1 = ((bf16[32,288,128]{2,1,0:T(8,128)(2,1)}), bf16[32,288,128]{2,1,0:T(8,128)(2,1)}, u32[]{:S(2)}, u32[]{:S(2)}) async-start(bf16[32,288,128]{2,1,0:T(8,128)(2,1)} %shard_map.58), calls=%async_computation.1 | async-start | bytes 4718592 | tf_op jit(solution)/shard_map/all_to_all | solution.py:259
Sparse Core Ops, SparseCore 0:
  9.1 166.5 all-gather.2
  177.5 45.7 all-gather.4

commit v2 on v1

v2 whole, which is shorter than its diff:
```python
import functools

import jax
import jax.numpy as jnp
from jax import lax
from jax.experimental import pallas as pl
from jax.experimental.pallas import tpu as pltpu
from jax.sharding import PartitionSpec as P

FF = 768
EXPERTS = 32
CAP = 18
MAIN = 16
GROUP = 8
SPILL = CAP - MAIN
LANES = 128
MIB = 1024 * 1024


def iota(shape, axis):
    return lax.broadcasted_iota(jnp.int32, shape, axis)


def dot(a, b):
    return jnp.dot(a, b, preferred_element_type=jnp.float32)


def as_bf16(mask):
    return mask.astype(jnp.float32).astype(jnp.bfloat16)


def spill_select(transposed):
    size = EXPERTS * MAIN
    row, col = iota((size, size), 0), iota((size, size), 1)
    if transposed:
        row, col = col, row
    return as_bf16(col == ((row & 63) >> 1) * MAIN + (row >> 6) * SPILL + (row & 1))


def row_of(block):
    return block // GROUP * GROUP * CAP + block % GROUP * MAIN


def spill_row_of(group):
    return group * GROUP * CAP + GROUP * MAIN


def dispatch_kernel(ids_ref, gates_ref, tokens_ref, out_ref, mix_ref, mix_spill_ref, select_ref, pack_ref):
    select_ref[...] = spill_select(False)
    pack_ref[...] = spill_select(True)
    rows, top = ids_ref.shape
    named = jnp.zeros((rows, EXPERTS), jnp.float32)
    gates = jnp.zeros((rows, EXPERTS), jnp.float32)
    for k in range(top):
        hit = ids_ref[:, k : k + 1] == iota((rows, EXPERTS), 1)
        named = named + hit.astype(jnp.float32)
        gates = gates + jnp.where(hit, gates_ref[:, k : k + 1], 0.0)
    named16 = named.astype(jnp.bfloat16)
    row, col = iota((rows, rows), 0), iota((rows, rows), 1)
    slots = dot(as_bf16(col < row), named16)
    over_tokens = (((0,), (0,)), ((), ()))
    named_t = lax.dot_general(named16, as_bf16(row == col), over_tokens, preferred_element_type=jnp.float32)
    slots_t = lax.dot_general(named16, as_bf16(row < col), over_tokens, preferred_element_type=jnp.float32)
    slots_t = jnp.where(named_t > 0.5, slots_t, -1.0)
    wide = jnp.broadcast_to(slots_t[:, None, :], (EXPERTS, MAIN, rows)).reshape(EXPERTS * MAIN, rows)
    place = iota((EXPERTS * MAIN, rows), 0) % MAIN
    pick = as_bf16(wide == place.astype(jnp.float32))
    width = tokens_ref.shape[1]
    blocks = width // LANES
    for b in range(0, blocks, 2):
        part = dot(pick, tokens_ref[:, b * LANES : (b + 2) * LANES]).astype(jnp.bfloat16)
        for i in range(2):
            start = row_of(b + i)
            out_ref[:, start : start + MAIN, :] = part[:, i * LANES : (i + 1) * LANES].reshape(EXPERTS, MAIN, LANES)
    picks = [
        as_bf16((place // SPILL == i) & (wide == (MAIN + place % SPILL).astype(jnp.float32))) for i in range(8)
    ]
    for g in range(blocks // 8):
        part = jnp.zeros((EXPERTS * MAIN, LANES), jnp.float32)
        for i in range(8):
            b = 8 * g + i
            part = part + dot(picks[i], tokens_ref[:, b * LANES : (b + 1) * LANES])
        start = spill_row_of(g)
        out_ref[:, start : start + MAIN, :] = part.astype(jnp.bfloat16).reshape(EXPERTS, MAIN, LANES)
    first = gates.astype(jnp.bfloat16)
    rest = gates - first.astype(jnp.float32)
    second = rest.astype(jnp.bfloat16)
    third = (rest - second.astype(jnp.float32)).astype(jnp.bfloat16)
    slots16 = slots.astype(jnp.bfloat16)
    for ref, per, base in ((mix_ref, MAIN, 0), (mix_spill_ref, SPILL, MAIN)):
        size = EXPERTS * per
        spread = as_bf16(iota((EXPERTS, size), 1) // per == iota((EXPERTS, size), 0))
        fits = dot(slots16, spread) == (base + iota((rows, size), 1) % per).astype(jnp.float32)
        for i, term in enumerate((first, second, third)):
            ref[i * rows : (i + 1) * rows, :] = jnp.where(fits, dot(term, spread), 0.0).astype(jnp.bfloat16)


def dispatch(ids, gates, tokens):
    rows, width = tokens.shape
    return pl.pallas_call(
        dispatch_kernel,
        out_shape=(
            jax.ShapeDtypeStruct((EXPERTS, CAP * width // LANES, LANES), jnp.bfloat16),
            jax.ShapeDtypeStruct((3 * rows, EXPERTS * MAIN), jnp.bfloat16),
            jax.ShapeDtypeStruct((3 * rows, EXPERTS * SPILL), jnp.bfloat16),
        )
        + (jax.ShapeDtypeStruct((EXPERTS * MAIN, EXPERTS * MAIN), jnp.bfloat16),) * 2,
        compiler_params=pltpu.CompilerParams(vmem_limit_bytes=60 * MIB),
    )(ids, gates, tokens)


def unpack_kernel(select_ref, in_ref, out_ref):
    size = EXPERTS * MAIN
    for b in range(GROUP):
        start = row_of(b)
        out_ref[:size, b * LANES : (b + 1) * LANES] = in_ref[:, start : start + MAIN, :].reshape(size, LANES)
    start = spill_row_of(0)
    part = dot(select_ref[...], in_ref[:, start : start + MAIN, :].reshape(size, LANES)).astype(jnp.bfloat16)
    for b in range(GROUP):
        out_ref[size:, b * LANES : (b + 1) * LANES] = part[b * 64 : (b + 1) * 64]


def unpack(select, incoming):
    groups = incoming.shape[1] // (GROUP * CAP)
    rows, step = EXPERTS * CAP, GROUP * LANES
    return pl.pallas_call(
        unpack_kernel,
        grid=(groups,),
        in_specs=[
            pl.BlockSpec(select.shape, lambda g: (0, 0)),
            pl.BlockSpec((EXPERTS, GROUP * CAP, LANES), lambda g: (0, g, 0)),
        ],
        out_specs=pl.BlockSpec((rows, step), lambda g: (0, g)),
        out_shape=jax.ShapeDtypeStruct((rows, groups * step), jnp.bfloat16),
        compiler_params=pltpu.CompilerParams(vmem_limit_bytes=60 * MIB),
    )(select, incoming)


def pack(part, out_ref, select):
    size = EXPERTS * MAIN
    for b in range(GROUP):
        start = row_of(b)
        out_ref[:, start : start + MAIN, :] = part[b // 2][:size, b % 2 * LANES : (b % 2 + 1) * LANES].reshape(
            EXPERTS, MAIN, LANES
        )
    spill = [part[b // 2][size:, b % 2 * LANES : (b % 2 + 1) * LANES] for b in range(GROUP)]
    moved = dot(select, jnp.concatenate(spill, axis=0)).astype(jnp.bfloat16)
    start = spill_row_of(0)
    out_ref[:, start : start + MAIN, :] = moved.reshape(EXPERTS, MAIN, LANES)


def gate_up_kernel(x_ref, weights_ref, hidden_ref, held_x, held, total, sems):
    bounds = [0, 512, 1536, 2560, held.shape[0]]
    chunks = len(bounds) - 1
    copies = []
    for i in range(chunks):
        at = pl.ds(bounds[i], bounds[i + 1] - bounds[i])
        copies.append(pltpu.make_async_copy(x_ref.at[:, at], held_x.at[:, at], sems.at[2 * i]))
        copies.append(pltpu.make_async_copy(weights_ref.at[0, at], held.at[at], sems.at[2 * i + 1]))
    for copy in copies:
        copy.start()
    step = 256
    for i in range(chunks):
        copies[2 * i].wait()
        copies[2 * i + 1].wait()
        at = slice(bounds[i], bounds[i + 1])
        for c in range(0, total.shape[1], step):
            part = dot(held_x[:, at], held[at, c : c + step])
            if i > 0:
                part = part + total[:, c : c + step]
            total[:, c : c + step] = part
    for c in range(0, FF, step):
        gate, up = total[:, c : c + step], total[:, FF + c : FF + c + step]
        hidden_ref[:, c : c + step] = (gate / (1.0 + jnp.exp(-gate)) * up).astype(jnp.bfloat16)


def gate_up_rows(x, weights):
    rows, width = x.shape
    return pl.pallas_call(
        gate_up_kernel,
        in_specs=[pl.BlockSpec(memory_space=pl.ANY)] * 2,
        out_specs=pl.BlockSpec(memory_space=pltpu.VMEM),
        out_shape=jax.ShapeDtypeStruct((rows, FF), jnp.bfloat16),
        scratch_shapes=[
            pltpu.VMEM((rows, width), jnp.bfloat16),
            pltpu.VMEM((width, 2 * FF), jnp.bfloat16),
            pltpu.VMEM((rows, 2 * FF), jnp.float32),
            pltpu.SemaphoreType.DMA((8,)),
        ],
        compiler_params=pltpu.CompilerParams(vmem_limit_bytes=60 * MIB),
    )(x, weights)


def first_kernel(places_ref, select_ref, hidden_ref, *refs):
    pieces, (out_ref, held, made, sems) = refs[:-4], refs[-4:]
    rows = pieces[0].shape[1]
    copies = []
    for i, piece in enumerate(pieces):
        at = pl.ds(pl.multiple_of(places_ref[i] * rows, 32), rows)
        copies.append(pltpu.make_async_copy(piece.at[0], held.at[at], sems.at[i]))
        copies[-1].start()
    for copy in copies:
        copy.wait()
    leaving = []
    for g in range(made.shape[0]):
        part = []
        for p in range(GROUP // 2):
            begin = (g * GROUP + 2 * p) * LANES
            part.append(dot(hidden_ref[...], held[:, begin : begin + 2 * LANES]).astype(jnp.bfloat16))
        pack(part, made.at[g], select_ref[...])
        at = pl.ds(g * GROUP * CAP, GROUP * CAP)
        leaving.append(pltpu.make_async_copy(made.at[g], out_ref.at[:, at], sems.at[len(pieces) + g]))
        leaving[-1].start()
    for copy in leaving:
        copy.wait()


def first_rows(places, select, hidden, pieces):
    depth, columns = pieces[0].shape[1:]
    count, groups = len(pieces), columns // (GROUP * LANES)
    vmem, smem = pl.BlockSpec(memory_space=pltpu.VMEM), pl.BlockSpec(memory_space=pltpu.SMEM)
    return pl.pallas_call(
        first_kernel,
        in_specs=[smem, vmem, vmem] + [pl.BlockSpec(memory_space=pl.ANY)] * count,
        out_specs=pl.BlockSpec(memory_space=pl.ANY),
        out_shape=jax.ShapeDtypeStruct((EXPERTS, groups * GROUP * CAP, LANES), jnp.bfloat16),
        scratch_shapes=[
            pltpu.VMEM((count * depth, columns), jnp.bfloat16),
            pltpu.VMEM((groups, EXPERTS, GROUP * CAP, LANES), jnp.bfloat16),
            pltpu.SemaphoreType.DMA((count + groups,)),
        ],
        compiler_params=pltpu.CompilerParams(vmem_limit_bytes=60 * MIB),
    )(places, select, hidden, *pieces)


def down_kernel(select_ref, hidden_ref, weights_ref, out_ref):
    part = []
    for p in range(GROUP // 2):
        at = slice(2 * p * LANES, (2 * p + 2) * LANES)
        part.append(dot(hidden_ref[...], weights_ref[0, :, at]).astype(jnp.bfloat16))
    pack(part, out_ref, select_ref[...])


def down_rows(select, hidden, weights):
    depth, width = weights.shape[1:]
    step = GROUP * LANES
    return pl.pallas_call(
        down_kernel,
        grid=(width // step,),
        in_specs=[
            pl.BlockSpec(memory_space=pltpu.VMEM),
            pl.BlockSpec(memory_space=pltpu.VMEM),
            pl.BlockSpec((1, depth, step), lambda g: (0, 0, g)),
        ],
        out_specs=pl.BlockSpec((EXPERTS, GROUP * CAP, LANES), lambda g: (0, g, 0)),
        out_shape=jax.ShapeDtypeStruct((EXPERTS, width // LANES * CAP, LANES), jnp.bfloat16),
        compiler_params=pltpu.CompilerParams(vmem_limit_bytes=60 * MIB),
    )(select, hidden, weights)


def combine_kernel(mix_ref, mix_spill_ref, select_ref, in_ref, *refs):
    out_ref = refs[-1]
    size = EXPERTS * MAIN
    rows = out_ref.shape[0]
    start = spill_row_of(0)
    spill = dot(select_ref[...], in_ref[:, start : start + MAIN, :].reshape(size, LANES)).astype(jnp.bfloat16)
    for p in range(GROUP // 2):
        main, extra = [], []
        for b in (2 * p, 2 * p + 1):
            start = row_of(b)
            main.append(in_ref[:, start : start + MAIN, :].reshape(size, LANES))
            extra.append(spill[b * 64 : (b + 1) * 64])
        total = dot(mix_ref[...], jnp.concatenate(main, axis=1))
        total = total + dot(mix_spill_ref[...], jnp.concatenate(extra, axis=1))
        total = total[2 * rows :] + total[rows : 2 * rows] + total[:rows]
        out_ref[:, 2 * p * LANES : (2 * p + 2) * LANES] = total.astype(jnp.bfloat16)


def combine(mix, mix_spill, select, returned, width, first, earlier):
    step = GROUP * LANES
    whole = pl.BlockSpec(memory_space=pltpu.VMEM)
    return pl.pallas_call(
        combine_kernel,
        grid=(returned.shape[1] // (GROUP * CAP),),
        in_specs=[whole] * 3
        + [pl.BlockSpec((EXPERTS, GROUP * CAP, LANES), lambda g: (0, g, 0))]
        + [pl.BlockSpec(memory_space=pl.ANY)] * len(earlier),
        out_specs=pl.BlockSpec((mix.shape[0] // 3, step), lambda g: (0, first + g)),
        out_shape=jax.ShapeDtypeStruct((mix.shape[0] // 3, width), jnp.bfloat16),
        input_output_aliases={4: 0} if earlier else {},
        compiler_params=pltpu.CompilerParams(vmem_limit_bytes=60 * MIB),
    )(mix, mix_spill, select, returned, *earlier)


STEPS = {1: 4, -1: 3}


def tie(value, others):
    return lax.optimization_barrier((value, tuple(others)))[0]


def body(tokens, expert_ids, gate_scale, gate_up, down):
    n, me = lax.axis_size("fsdp"), lax.axis_index("fsdp")
    split = down.shape[2] // 2
    weights = lax.all_gather(gate_up, "fsdp", axis=1, tiled=True)
    gathered = lax.all_gather(down[:, :, split:], "fsdp", axis=1, tiled=True)
    own = down[:, :, :split]
    pieces, shards = [own], [me]
    latest = {way: own for way in STEPS}

    def step(k):
        for way, steps in STEPS.items():
            if k <= steps:
                latest[way] = lax.ppermute(latest[way], "fsdp", [(j, (j + way) % n) for j in range(n)])
                pieces.append(latest[way])
                shards.append((me - way * k + n) % n)

    step(1)
    tokens = tie(tokens, pieces[1:])
    outgoing, mix, mix_spill, select, packing = dispatch(expert_ids, gate_scale, tokens)
    incoming = lax.all_to_all(outgoing, "expert", split_axis=0, concat_axis=0, tiled=True)
    x = unpack(select, incoming)
    step(2)
    step(3)
    weights, x, latest[1] = lax.optimization_barrier((weights, tie(x, pieces[1:]), latest[1]))
    step(4)
    hidden = gate_up_rows(x, weights)

    result = []
    for part in range(2):
        if part == 0:
            rows = first_rows(jnp.stack(shards).astype(jnp.int32), packing, hidden, pieces)
        else:
            rows = down_rows(packing, hidden, gathered)
        returned = lax.all_to_all(rows, "expert", split_axis=0, concat_axis=0, tiled=True)
        first = part * split // (GROUP * LANES)
        result = [combine(mix, mix_spill, select, returned, down.shape[2], first, result)]
    return result[0]


def solution(mesh):
    return jax.shard_map(
        body,
        mesh=mesh,
        in_specs=(
            P(("fsdp", "expert"), None),
            P(("fsdp", "expert"), None),
            P(("fsdp", "expert"), None),
            P("expert", "fsdp", None),
            P("expert", "fsdp", None),
        ),
        out_specs=P(("fsdp", "expert"), None),
        check_vma=False,
    )
```

time: 287 us -> 271 us (0.944)
  waiting for transfers between devices: 187 us -> 179 us
  Pallas kernels: 47.6 us -> 43.8 us
    all_to_all x1, waiting for transfers between devices: 0.01 us -> 35.8 us  [body(): lax.all_to_all(outgoing, 'expert', split_axis=0, concat_axis=0, tiled=True)]
    ppermute x7, waiting for transfers between devices: 62.3 us -> 28.1 us  [step(): lax.ppermute(latest[way], 'fsdp', [(j, (j + way) % n) for j in range(n)])]
    all_gather x1, waiting for transfers between devices: 69.5 us -> 56.7 us  [body(): weights = lax.all_gather(gate_up, 'fsdp', axis=1, tiled=True)]
    all_to_all x2, waiting for transfers between devices: 34.1 us -> 39.3 us  [body(): lax.all_to_all(rows, 'expert', split_axis=0, concat_axis=0, tiled=True)]
    pallas_call x6, Pallas kernels: 41.3 us -> 37 us  [the longest x1 10.9 us: gate_up_rows(): pl.pallas_call(gate_up_kernel, in_specs=[pl.BlockSpec(memory_space=pl.ANY...]
    all_gather x1, waiting for transfers between devices: 20.8 us -> 17.5 us  [body(): gathered = lax.all_gather(down[:, :, split:], 'fsdp', axis=1, tiled=True)]
  transfers between devices with their start and end apart: 12 -> 12, of which waited for: 10 -> 8; matrix products, arithmetic and copies ran while one was open for 1% -> 1% of each run, Pallas kernels for 15% -> 15%
where the time goes in v2:
time: 271 us
  waiting for transfers between devices  179 us (66%)
  Pallas kernels  43.8 us (16%)
  starting transfers between devices  29.7 us (11%)
  between operations  13.5 us (5%)
  local copies, waits for them, and re-layouts  4.75 us (2%)
    all_gather x1, waiting for transfers between devices, body(): weights = lax.all_gather(gate_up, 'fsdp', axis=1, tiled=True)  56.7 us
    all_to_all x2, waiting for transfers between devices, body(): lax.all_to_all(rows, 'expert', split_axis=0, concat_axis=0, tiled=True)  39.3 us
    all_to_all x1, waiting for transfers between devices, body(): lax.all_to_all(outgoing, 'expert', split_axis=0, concat_axis=0, tiled=True)  35.8 us
    ppermute x7, waiting for transfers between devices, step(): lax.ppermute(latest[way], 'fsdp', [(j, (j + way) % n) for j in range(n)])  28.1 us
    all_gather x1, waiting for transfers between devices, body(): gathered = lax.all_gather(down[:, :, split:], 'fsdp', axis=1, tiled=True)  17.5 us
    all_to_all x2, starting transfers between devices, body(): lax.all_to_all(rows, 'expert', split_axis=0, concat_axis=0, tiled=True)  11.9 us
    pallas_call x1, Pallas kernels, gate_up_rows(): pl.pallas_call(gate_up_kernel, in_specs=[pl.BlockSpec(memory_space=pl.ANY...  10.9 us
    ppermute x7, starting transfers between devices, step(): lax.ppermute(latest[way], 'fsdp', [(j, (j + way) % n) for j in range(n)])  10.3 us
  transfers between devices with their start and end apart: 12, of which 8 were waited for; matrix products, arithmetic and copies ran while one was open for 1% of the time, Pallas kernels for 15%

profile of v2, /device:TPU:64, one launch (start us, length us, event | category | flops | bytes accessed | tf_op | source)
XLA Modules:
  0.0 270.6 jit_solution(12924003215462692105)
XLA Ops:
  6.5 0.0 copy-start.9
  6.5 0.0 copy-start.10
  6.5 0.0 all-gather.3.cloned.1.call-start
  6.5 0.7 all-gather.3.cloned.1.call-update
  7.3 1.9 fusion
  9.2 0.0 copy-start.1
  9.2 1.9 collective-permute-start
  11.1 0.1 collective-permute-start.1
  11.2 0.0 copy-done.9
  11.2 0.7 copy.7.ids_ref
  11.9 0.0 copy-done.10
  11.9 0.7 copy.8.gates_ref
  12.6 7.5 %collective-permute-done.refs_1_ = bf16[1,96,2048]{2,1,0:T(8,128)(2,1)S(1)} collective-permute-done((bf16[1,96,2048]{2,1,0:T(8,128)(2,1)S(1)}, bf16[1,96,2048]{2,1,0:T(8,128)(2,1)S(1)}, u32[]{:S(2)}, u32[]{:S(2)}) %collective-permute-start) | collective-permute-done | bytes 393248 | tf_op jit(solution)/shard_map/ppermute | solution.py:314
  20.0 0.0 copy-start.2
  20.0 3.0 %collective-permute-done.1.refs_2_ = bf16[1,96,2048]{2,1,0:T(8,128)(2,1)S(1)} collective-permute-done((bf16[1,96,2048]{2,1,0:T(8,128)(2,1)S(1)}, bf16[1,96,2048]{2,1,0:T(8,128)(2,1)S(1)}, u32[]{:S(2)}, u32[]{:S(2)}) %collective-permute-start.1) | collective-permute-done | bytes 393248 | tf_op jit(solution)/shard_map/ppermute | solution.py:314
  23.1 0.0 copy-start.3
  23.1 6.7 %shard_map.55 = (bf16[32,576,128]{2,1,0:T(8,128)(2,1)}, bf16[144,512]{1,0:T(8,128)(2,1)}, bf16[144,64]{1,0:T(8,128)(2,1)}, bf16[512,512]{1,0:T(8,128)(2,1)}, bf16[512,512]{1,0:T(8,128)(2,1)}) custom-call(s32[48,8]{1,0:T(8,128)} %copy.7.ids_ref, f32[48,8]{1,0:T(8,128)} %copy.8.gates_ref, bf16[48,4096]{1,0:T(8,128)(2,1)} %tokens_ref), custom_call_target="tpu_custom_call" | custom-call | tf_op jit(solution)/shard_map/pallas_call | solution.py:100
  29.8 0.0 copy-done.1
  29.8 7.4 %all-to-all-start = ((bf16[32,576,128]{2,1,0:T(8,128)(2,1)}), bf16[32,576,128]{2,1,0:T(8,128)(2,1)}, u32[]{:S(2)}, u32[]{:S(2)}) async-start(bf16[32,576,128]{2,1,0:T(8,128)(2,1)} %get-tuple-element.20), calls=%async_computation | async-start | bytes 9437184 | tf_op jit(solution)/shard_map/all_to_all | solution.py:321
  37.3 0.0 all-gather.5.cloned.1.call-start
  37.3 0.7 all-gather.5.cloned.1.call-update
  38.0 0.0 copy-done.2
  38.0 3.0 %collective-permute-start.2 = (bf16[1,96,2048]{2,1,0:T(8,128)(2,1)S(1)}, bf16[1,96,2048]{2,1,0:T(8,128)(2,1)S(1)}, u32[]{:S(2)}, u32[]{:S(2)}) collective-permute-start(bf16[1,96,2048]{2,1,0:T(8,128)(2,1)S(1)} %collective-permute-done.refs_1_), channel_id=1, source_target_pairs={{0,32},{32,64},{64,96},{96,128},{128,160},{160,192},{192,224},{224... | collective-permute-start | bytes 1179656 | tf_op jit(solution)/shard_map/ppermute | solution.py:314
  41.0 0.0 copy-done.3
  41.0 0.0 collective-permute-start.3
  41.0 17.6 %collective-permute-done.2.refs_3_ = bf16[1,96,2048]{2,1,0:T(8,128)(2,1)S(1)} collective-permute-done((bf16[1,96,2048]{2,1,0:T(8,128)(2,1)S(1)}, bf16[1,96,2048]{2,1,0:T(8,128)(2,1)S(1)}, u32[]{:S(2)}, u32[]{:S(2)}) %collective-permute-start.2) | collective-permute-done | bytes 393248 | tf_op jit(solution)/shard_map/ppermute | solution.py:314
  58.7 0.0 copy-start.4
  58.7 2.5 collective-permute-start.4
  61.2 0.0 collective-permute-done.3.refs_4_
  61.2 0.0 copy-start.5
  61.2 0.0 collective-permute-start.5
  61.2 35.8 %all-to-all-done.in_ref = bf16[32,576,128]{2,1,0:T(8,128)(2,1)} async-done(((bf16[32,576,128]{2,1,0:T(8,128)(2,1)}), bf16[32,576,128]{2,1,0:T(8,128)(2,1)}, u32[]{:S(2)}, u32[]{:S(2)}) %all-to-all-start) | async-done | bytes 4718624 | tf_op jit(solution)/shard_map/all_to_all | solution.py:321
  97.0 6.2 %shard_map.56.x_ref = bf16[576,4096]{1,0:T(8,128)(2,1)} custom-call(bf16[512,512]{1,0:T(8,128)(2,1)} %get-tuple-element.18.select_ref, bf16[32,576,128]{2,1,0:T(8,128)(2,1)} %all-to-all-done.in_ref), custom_call_target="tpu_custom_call" | custom-call | tf_op jit(solution)/shard_map/pallas_call | solution.py:126
  103.2 0.0 copy-done.4
  103.2 0.0 copy-done.5
  103.2 0.0 collective-permute-done.4.refs_5_
  103.2 0.0 copy-start.6
  103.2 0.0 collective-permute-done.5.refs_6_
  103.2 0.0 copy-start.7
  103.2 56.7 %all-gather.3.cloned.1.call-done.weights_ref = bf16[1,4096,1536]{2,1,0:T(8,128)(2,1)} async-done(((bf16[1,512,1536]{2,1,0:T(8,128)(2,1)}), bf16[1,4096,1536]{2,1,0:T(8,128)(2,1)}) %all-gather.3.cloned.1.call-update) | async-done | bytes 12582928 | tf_op jit(solution)/shard_map/all_gather | solution.py:305
  160.0 2.8 %collective-permute-start.6 = (bf16[1,96,2048]{2,1,0:T(8,128)(2,1)S(1)}, bf16[1,96,2048]{2,1,0:T(8,128)(2,1)S(1)}, u32[]{:S(2)}, u32[]{:S(2)}) collective-permute-start(bf16[1,96,2048]{2,1,0:T(8,128)(2,1)S(1)} %collective-permute-done.4.refs_5_), channel_id=1, source_target_pairs={{0,32},{32,64},{64,96},{96,128},{128,160},{160,192},{192,224},{224... | collective-permute-start | bytes 1179656 | tf_op jit(solution)/shard_map/ppermute | solution.py:314
  162.7 0.7 stack.35.places_ref
  163.4 10.9 %shard_map.57.hidden_ref = bf16[576,768]{1,0:T(8,128)(2,1)} custom-call(bf16[576,4096]{1,0:T(8,128)(2,1)} %shard_map.56.x_ref, bf16[1,4096,1536]{2,1,0:T(8,128)(2,1)} %all-gather.3.cloned.1.call-done.weights_ref), custom_call_target="tpu_custom_call" | custom-call | tf_op jit(solution)/shard_map/pallas_call | solution.py:179
  174.3 0.0 copy-done.6
  174.3 0.0 copy-done.7
  174.3 0.0 collective-permute-done.6.refs_7_
  174.3 0.0 copy-start.8
  174.3 0.8 copy-done.8
  175.1 6.8 %shard_map.59 = bf16[32,288,128]{2,1,0:T(8,128)(2,1)} custom-call(s32[8]{0:T(128)} %stack.35.places_ref, bf16[512,512]{1,0:T(8,128)(2,1)} %get-tuple-element.19.select_ref, bf16[576,768]{1,0:T(8,128)(2,1)} %shard_map.57.hidden_ref, bf16[1,96,2048]{2,1,0:T(8,128)(2,1)} %copy-done.1, bf16[1,96,2048]{2,1,0:T(8,128)(2,1)} %copy-done.2, ...), custom_call_target="tpu_custom_call" | custom-call | tf_op jit(solution)/shard_map/pallas_call | solution.py:222
  181.9 7.1 %all-to-all-start.2 = ((bf16[32,288,128]{2,1,0:T(8,128)(2,1)}), bf16[32,288,128]{2,1,0:T(8,128)(2,1)S(1)}, u32[]{:S(2)}, u32[]{:S(2)}) async-start(bf16[32,288,128]{2,1,0:T(8,128)(2,1)} %shard_map.59), calls=%async_computation.2 | async-start | bytes 4718592 | tf_op jit(solution)/shard_map/all_to_all | solution.py:335
  189.1 17.5 %all-gather.5.cloned.1.call-done.weights_ref = bf16[1,768,2048]{2,1,0:T(8,128)(2,1)} async-done(((bf16[1,96,2048]{2,1,0:T(8,128)(2,1)}), bf16[1,768,2048]{2,1,0:T(8,128)(2,1)}) %all-gather.5.cloned.1.call-update) | async-done | bytes 3145744 | tf_op jit(solution)/shard_map/all_gather | solution.py:306
  206.5 5.6 %shard_map.58 = bf16[32,288,128]{2,1,0:T(8,128)(2,1)} custom-call(bf16[512,512]{1,0:T(8,128)(2,1)} %get-tuple-element.19.select_ref, bf16[576,768]{1,0:T(8,128)(2,1)} %shard_map.57.hidden_ref, bf16[1,768,2048]{2,1,0:T(8,128)(2,1)} %all-gather.5.cloned.1.call-done.weights_ref), custom_call_target="tpu_custom_call" | custom-call | tf_op jit(solution)/shard_map/pallas_call | solution.py:247
  212.1 10.0 %all-to-all-done.2.in_ref = bf16[32,288,128]{2,1,0:T(8,128)(2,1)S(1)} async-done(((bf16[32,288,128]{2,1,0:T(8,128)(2,1)}), bf16[32,288,128]{2,1,0:T(8,128)(2,1)S(1)}, u32[]{:S(2)}, u32[]{:S(2)}) %all-to-all-start.2) | async-done | bytes 2359328 | tf_op jit(solution)/shard_map/all_to_all | solution.py:335
  222.1 0.0 copy-start
  222.1 4.8 %all-to-all-start.1 = ((bf16[32,288,128]{2,1,0:T(8,128)(2,1)}), bf16[32,288,128]{2,1,0:T(8,128)(2,1)}, u32[]{:S(2)}, u32[]{:S(2)}) async-start(bf16[32,288,128]{2,1,0:T(8,128)(2,1)} %shard_map.58), calls=%async_computation.1 | async-start | bytes 4718592 | tf_op jit(solution)/shard_map/all_to_all | solution.py:335
  227.0 0.0 copy-done
  227.0 3.8 %shard_map.60.refs_0_ = bf16[48,4096]{1,0:T(8,128)(2,1)} custom-call(bf16[144,512]{1,0:T(8,128)(2,1)} %get-tuple-element.16.mix_ref, bf16[144,64]{1,0:T(8,128)(2,1)} %get-tuple-element.17.mix_spill_ref, bf16[512,512]{1,0:T(8,128)(2,1)} %get-tuple-element.18.select_ref, bf16[32,288,128]{2,1,0:T(8,128)(2,1)} %copy-done), custom_call_target="tpu_custom_call" | custom-call | tf_op jit(solution)/shard_map/pallas_call | solution.py:282
  230.8 29.3 %all-to-all-done.1.in_ref = bf16[32,288,128]{2,1,0:T(8,128)(2,1)} async-done(((bf16[32,288,128]{2,1,0:T(8,128)(2,1)}), bf16[32,288,128]{2,1,0:T(8,128)(2,1)}, u32[]{:S(2)}, u32[]{:S(2)}) %all-to-all-start.1) | async-done | bytes 2359328 | tf_op jit(solution)/shard_map/all_to_all | solution.py:335
  260.0 3.8 %shard_map.61 = bf16[48,4096]{1,0:T(8,128)(2,1)} custom-call(bf16[144,512]{1,0:T(8,128)(2,1)} %get-tuple-element.16.mix_ref, bf16[144,64]{1,0:T(8,128)(2,1)} %get-tuple-element.17.mix_spill_ref, bf16[512,512]{1,0:T(8,128)(2,1)} %get-tuple-element.18.select_ref, bf16[32,288,128]{2,1,0:T(8,128)(2,1)} %all-to-all-done.1.in_ref, ...), custom_call_target="tpu_custom_call", output_to_operand_aliasing={{}: (4, {})} | custom-call | tf_op jit(solution)/shard_map/pallas_call | solution.py:282
Async XLA Ops:
  6.5 4.7 %copy-start.9 = (s32[48,8]{0,1:T(8,128)S(1)}, s32[48,8]{0,1:T(8,128)}, u32[]{:S(2)}) copy-start(s32[48,8]{0,1:T(8,128)} %param.6) | copy-start | bytes 4612
  6.5 5.4 %copy-start.10 = (f32[48,8]{0,1:T(8,128)S(1)}, f32[48,8]{0,1:T(8,128)}, u32[]{:S(2)}) copy-start(f32[48,8]{0,1:T(8,128)} %param.7) | copy-start | bytes 4612
  6.5 153.4 %all-gather.3.cloned.1.call-start = ((), (), s32[]{:S(2)}) async-start(), calls=%async_computation.3 | async-start | bytes 14155776 | tf_op jit(solution)/shard_map/all_gather | solution.py:305
  9.2 20.6 %copy-start.1 = (bf16[1,96,2048]{2,1,0:T(8,128)(2,1)}, bf16[1,96,2048]{2,1,0:T(8,128)(2,1)S(1)}, u32[]{:S(2)}) copy-start(bf16[1,96,2048]{2,1,0:T(8,128)(2,1)S(1)} %get-tuple-element.26.refs_0_) | copy-start | bytes 1179652
  9.2 10.9 %collective-permute-start = (bf16[1,96,2048]{2,1,0:T(8,128)(2,1)S(1)}, bf16[1,96,2048]{2,1,0:T(8,128)(2,1)S(1)}, u32[]{:S(2)}, u32[]{:S(2)}) collective-permute-start(bf16[1,96,2048]{2,1,0:T(8,128)(2,1)S(1)} %get-tuple-element.26.refs_0_), channel_id=1, source_target_pairs={{0,32},{32,64},{64,96},{96,128},{128,160},{160,192},{192,224},{224... | collective-permute-start | bytes 1179656 | tf_op jit(solution)/shard_map/ppermute | solution.py:314
  11.1 12.0 %collective-permute-start.1 = (bf16[1,96,2048]{2,1,0:T(8,128)(2,1)S(1)}, bf16[1,96,2048]{2,1,0:T(8,128)(2,1)S(1)}, u32[]{:S(2)}, u32[]{:S(2)}) collective-permute-start(bf16[1,96,2048]{2,1,0:T(8,128)(2,1)S(1)} %get-tuple-element.26.refs_0_), channel_id=1, source_target_pairs={{0,224},{32,0},{64,32},{96,64},{128,96},{160,128},{192,160},{224,1... | collective-permute-start | bytes 1179656 | tf_op jit(solution)/shard_map/ppermute | solution.py:314
  20.0 18.0 %copy-start.2 = (bf16[1,96,2048]{2,1,0:T(8,128)(2,1)}, bf16[1,96,2048]{2,1,0:T(8,128)(2,1)S(1)}, u32[]{:S(2)}) copy-start(bf16[1,96,2048]{2,1,0:T(8,128)(2,1)S(1)} %collective-permute-done.refs_1_) | copy-start | bytes 1179652
  23.1 18.0 %copy-start.3 = (bf16[1,96,2048]{2,1,0:T(8,128)(2,1)}, bf16[1,96,2048]{2,1,0:T(8,128)(2,1)S(1)}, u32[]{:S(2)}) copy-start(bf16[1,96,2048]{2,1,0:T(8,128)(2,1)S(1)} %collective-permute-done.1.refs_2_) | copy-start | bytes 1179652
  29.8 67.2 %all-to-all-start = ((bf16[32,576,128]{2,1,0:T(8,128)(2,1)}), bf16[32,576,128]{2,1,0:T(8,128)(2,1)}, u32[]{:S(2)}, u32[]{:S(2)}) async-start(bf16[32,576,128]{2,1,0:T(8,128)(2,1)} %get-tuple-element.20), calls=%async_computation | async-start | bytes 9437184 | tf_op jit(solution)/shard_map/all_to_all | solution.py:321
  37.3 169.3 %all-gather.5.cloned.1.call-start = ((), (), s32[]{:S(2)}) async-start(), calls=%async_computation.4 | async-start | bytes 3538944 | tf_op jit(solution)/shard_map/all_gather | solution.py:306
  38.0 20.6 %collective-permute-start.2 = (bf16[1,96,2048]{2,1,0:T(8,128)(2,1)S(1)}, bf16[1,96,2048]{2,1,0:T(8,128)(2,1)S(1)}, u32[]{:S(2)}, u32[]{:S(2)}) collective-permute-start(bf16[1,96,2048]{2,1,0:T(8,128)(2,1)S(1)} %collective-permute-done.refs_1_), channel_id=1, source_target_pairs={{0,32},{32,64},{64,96},{96,128},{128,160},{160,192},{192,224},{224... | collective-permute-start | bytes 1179656 | tf_op jit(solution)/shard_map/ppermute | solution.py:314
  41.0 20.1 %collective-permute-start.3 = (bf16[1,96,2048]{2,1,0:T(8,128)(2,1)S(1)}, bf16[1,96,2048]{2,1,0:T(8,128)(2,1)S(1)}, u32[]{:S(2)}, u32[]{:S(2)}) collective-permute-start(bf16[1,96,2048]{2,1,0:T(8,128)(2,1)S(1)} %collective-permute-done.1.refs_2_), channel_id=1, source_target_pairs={{0,224},{32,0},{64,32},{96,64},{128,96},{160,128},{192,160},{224,1... | collective-permute-start | bytes 1179656 | tf_op jit(solution)/shard_map/ppermute | solution.py:314
  58.7 44.5 %copy-start.4 = (bf16[1,96,2048]{2,1,0:T(8,128)(2,1)}, bf16[1,96,2048]{2,1,0:T(8,128)(2,1)S(1)}, u32[]{:S(2)}) copy-start(bf16[1,96,2048]{2,1,0:T(8,128)(2,1)S(1)} %collective-permute-done.2.refs_3_) | copy-start | bytes 1179652
  58.7 44.5 %collective-permute-start.4 = (bf16[1,96,2048]{2,1,0:T(8,128)(2,1)S(1)}, bf16[1,96,2048]{2,1,0:T(8,128)(2,1)S(1)}, u32[]{:S(2)}, u32[]{:S(2)}) collective-permute-start(bf16[1,96,2048]{2,1,0:T(8,128)(2,1)S(1)} %collective-permute-done.2.refs_3_), channel_id=1, source_target_pairs={{0,32},{32,64},{64,96},{96,128},{128,160},{160,192},{192,224},{224... | collective-permute-start | bytes 1179656 | tf_op jit(solution)/shard_map/ppermute | solution.py:314
  61.2 42.0 %copy-start.5 = (bf16[1,96,2048]{2,1,0:T(8,128)(2,1)}, bf16[1,96,2048]{2,1,0:T(8,128)(2,1)S(1)}, u32[]{:S(2)}) copy-start(bf16[1,96,2048]{2,1,0:T(8,128)(2,1)S(1)} %collective-permute-done.3.refs_4_) | copy-start | bytes 1179652
  61.2 42.1 %collective-permute-start.5 = (bf16[1,96,2048]{2,1,0:T(8,128)(2,1)S(1)}, bf16[1,96,2048]{2,1,0:T(8,128)(2,1)S(1)}, u32[]{:S(2)}, u32[]{:S(2)}) collective-permute-start(bf16[1,96,2048]{2,1,0:T(8,128)(2,1)S(1)} %collective-permute-done.3.refs_4_), channel_id=1, source_target_pairs={{0,224},{32,0},{64,32},{96,64},{128,96},{160,128},{192,160},{224,1... | collective-permute-start | bytes 1179656 | tf_op jit(solution)/shard_map/ppermute | solution.py:314
  103.2 71.1 %copy-start.6 = (bf16[1,96,2048]{2,1,0:T(8,128)(2,1)}, bf16[1,96,2048]{2,1,0:T(8,128)(2,1)S(1)}, u32[]{:S(2)}) copy-start(bf16[1,96,2048]{2,1,0:T(8,128)(2,1)S(1)} %collective-permute-done.4.refs_5_) | copy-start | bytes 1179652
  103.2 71.1 %copy-start.7 = (bf16[1,96,2048]{2,1,0:T(8,128)(2,1)}, bf16[1,96,2048]{2,1,0:T(8,128)(2,1)S(1)}, u32[]{:S(2)}) copy-start(bf16[1,96,2048]{2,1,0:T(8,128)(2,1)S(1)} %collective-permute-done.5.refs_6_) | copy-start | bytes 1179652
  160.0 14.4 %collective-permute-start.6 = (bf16[1,96,2048]{2,1,0:T(8,128)(2,1)S(1)}, bf16[1,96,2048]{2,1,0:T(8,128)(2,1)S(1)}, u32[]{:S(2)}, u32[]{:S(2)}) collective-permute-start(bf16[1,96,2048]{2,1,0:T(8,128)(2,1)S(1)} %collective-permute-done.4.refs_5_), channel_id=1, source_target_pairs={{0,32},{32,64},{64,96},{96,128},{128,160},{160,192},{192,224},{224... | collective-permute-start | bytes 1179656 | tf_op jit(solution)/shard_map/ppermute | solution.py:314
  174.3 0.8 copy-start.8
  181.9 40.2 %all-to-all-start.2 = ((bf16[32,288,128]{2,1,0:T(8,128)(2,1)}), bf16[32,288,128]{2,1,0:T(8,128)(2,1)S(1)}, u32[]{:S(2)}, u32[]{:S(2)}) async-start(bf16[32,288,128]{2,1,0:T(8,128)(2,1)} %shard_map.59), calls=%async_computation.2 | async-start | bytes 4718592 | tf_op jit(solution)/shard_map/all_to_all | solution.py:335
  222.1 4.8 %copy-start = (bf16[32,288,128]{2,1,0:T(8,128)(2,1)}, bf16[32,288,128]{2,1,0:T(8,128)(2,1)S(1)}, u32[]{:S(2)}) copy-start(bf16[32,288,128]{2,1,0:T(8,128)(2,1)S(1)} %all-to-all-done.2.in_ref) | copy-start | bytes 7077892
  222.1 37.9 %all-to-all-start.1 = ((bf16[32,288,128]{2,1,0:T(8,128)(2,1)}), bf16[32,288,128]{2,1,0:T(8,128)(2,1)}, u32[]{:S(2)}, u32[]{:S(2)}) async-start(bf16[32,288,128]{2,1,0:T(8,128)(2,1)} %shard_map.58), calls=%async_computation.1 | async-start | bytes 4718592 | tf_op jit(solution)/shard_map/all_to_all | solution.py:335
Sparse Core Ops, SparseCore 0:
  9.1 150.7 all-gather.2
  161.7 44.7 all-gather.4

commit v3 on v2

--- a/solution.py
+++ b/solution.py
@@ -150,7 +150,7 @@
 
 
 def gate_up_kernel(x_ref, weights_ref, hidden_ref, held_x, held, total, sems):
-    bounds = [0, 512, 1536, 2560, held.shape[0]]
+    bounds = [0, 256, 1024, 2048, 3072, held.shape[0]]
     chunks = len(bounds) - 1
     copies = []
     for i in range(chunks):
@@ -178,38 +178,50 @@
     rows, width = x.shape
     return pl.pallas_call(
         gate_up_kernel,
-        in_specs=[pl.BlockSpec(memory_space=pl.ANY)] * 2,
+        in_specs=[pl.BlockSpec(memory_space=pltpu.HBM)] * 2,
         out_specs=pl.BlockSpec(memory_space=pltpu.VMEM),
         out_shape=jax.ShapeDtypeStruct((rows, FF), jnp.bfloat16),
         scratch_shapes=[
             pltpu.VMEM((rows, width), jnp.bfloat16),
             pltpu.VMEM((width, 2 * FF), jnp.bfloat16),
             pltpu.VMEM((rows, 2 * FF), jnp.float32),
-            pltpu.SemaphoreType.DMA((8,)),
+            pltpu.SemaphoreType.DMA((10,)),
         ],
         compiler_params=pltpu.CompilerParams(vmem_limit_bytes=60 * MIB),
     )(x, weights)
 
 
 def first_kernel(places_ref, select_ref, hidden_ref, *refs):
-    pieces, (out_ref, held, made, sems) = refs[:-4], refs[-4:]
-    rows = pieces[0].shape[1]
+    pieces, (out_ref, held, made, held_hidden, held_select, sems, leave_sems) = refs[:-7], refs[-7:]
+    rows, width = pieces[0].shape[1], GROUP * LANES
+    groups = made.shape[0]
+    hidden_copy = pltpu.make_async_copy(hidden_ref, held_hidden, sems.at[groups, 0])
+    select_copy = pltpu.make_async_copy(select_ref, held_select, sems.at[groups, 1])
+    hidden_copy.start()
     copies = []
-    for i, piece in enumerate(pieces):
-        at = pl.ds(pl.multiple_of(places_ref[i] * rows, 32), rows)
-        copies.append(pltpu.make_async_copy(piece.at[0], held.at[at], sems.at[i]))
-        copies[-1].start()
-    for copy in copies:
-        copy.wait()
+    for g in range(groups):
+        cols = pl.ds(g * width, width)
+        copies.append([])
+        for i, piece in enumerate(pieces):
+            at = pl.ds(pl.multiple_of(places_ref[i] * rows, 32), rows)
+            copies[g].append(pltpu.make_async_copy(piece.at[0, :, cols], held.at[at, cols], sems.at[g, i]))
+            copies[g][-1].start()
+        if g == 0:
+            select_copy.start()
     leaving = []
-    for g in range(made.shape[0]):
+    hidden_copy.wait()
+    for g in range(groups):
+        for copy in copies[g]:
+            copy.wait()
         part = []
         for p in range(GROUP // 2):
             begin = (g * GROUP + 2 * p) * LANES
-            part.append(dot(hidden_ref[...], held[:, begin : begin + 2 * LANES]).astype(jnp.bfloat16))
-        pack(part, made.at[g], select_ref[...])
+            part.append(dot(held_hidden[...], held[:, begin : begin + 2 * LANES]).astype(jnp.bfloat16))
+        if g == 0:
+            select_copy.wait()
+        pack(part, made.at[g], held_select[...])
         at = pl.ds(g * GROUP * CAP, GROUP * CAP)
-        leaving.append(pltpu.make_async_copy(made.at[g], out_ref.at[:, at], sems.at[len(pieces) + g]))
+        leaving.append(pltpu.make_async_copy(made.at[g], out_ref.at[:, at], leave_sems.at[g]))
         leaving[-1].start()
     for copy in leaving:
         copy.wait()
@@ -218,16 +230,18 @@
 def first_rows(places, select, hidden, pieces):
     depth, columns = pieces[0].shape[1:]
     count, groups = len(pieces), columns // (GROUP * LANES)
-    vmem, smem = pl.BlockSpec(memory_space=pltpu.VMEM), pl.BlockSpec(memory_space=pltpu.SMEM)
     return pl.pallas_call(
         first_kernel,
-        in_specs=[smem, vmem, vmem] + [pl.BlockSpec(memory_space=pl.ANY)] * count,
+        in_specs=[pl.BlockSpec(memory_space=pltpu.SMEM)] + [pl.BlockSpec(memory_space=pl.ANY)] * (2 + count),
         out_specs=pl.BlockSpec(memory_space=pl.ANY),
         out_shape=jax.ShapeDtypeStruct((EXPERTS, groups * GROUP * CAP, LANES), jnp.bfloat16),
         scratch_shapes=[
             pltpu.VMEM((count * depth, columns), jnp.bfloat16),
             pltpu.VMEM((groups, EXPERTS, GROUP * CAP, LANES), jnp.bfloat16),
-            pltpu.SemaphoreType.DMA((count + groups,)),
+            pltpu.VMEM(hidden.shape, jnp.bfloat16),
+            pltpu.VMEM(select.shape, jnp.bfloat16),
+            pltpu.SemaphoreType.DMA((groups + 1, count)),
+            pltpu.SemaphoreType.DMA((groups,)),
         ],
         compiler_params=pltpu.CompilerParams(vmem_limit_bytes=60 * MIB),
     )(places, select, hidden, *pieces)
@@ -258,37 +272,53 @@
     )(select, hidden, weights)
 
 
-def combine_kernel(mix_ref, mix_spill_ref, select_ref, in_ref, *refs):
-    out_ref = refs[-1]
+def combine_kernel(first, mix_ref, mix_spill_ref, select_ref, in_ref, *refs):
+    out_ref, held, made, sems = refs[-4:]
+    groups = held.shape[0]
+    arriving, leaving = [], []
+    for g in range(groups):
+        at = pl.ds(g * GROUP * CAP, GROUP * CAP)
+        arriving.append(pltpu.make_async_copy(in_ref.at[:, at], held.at[g], sems.at[g]))
+        arriving[-1].start()
     size = EXPERTS * MAIN
-    rows = out_ref.shape[0]
-    start = spill_row_of(0)
-    spill = dot(select_ref[...], in_ref[:, start : start + MAIN, :].reshape(size, LANES)).astype(jnp.bfloat16)
-    for p in range(GROUP // 2):
-        main, extra = [], []
-        for b in (2 * p, 2 * p + 1):
-            start = row_of(b)
-            main.append(in_ref[:, start : start + MAIN, :].reshape(size, LANES))
-            extra.append(spill[b * 64 : (b + 1) * 64])
-        total = dot(mix_ref[...], jnp.concatenate(main, axis=1))
-        total = total + dot(mix_spill_ref[...], jnp.concatenate(extra, axis=1))
-        total = total[2 * rows :] + total[rows : 2 * rows] + total[:rows]
-        out_ref[:, 2 * p * LANES : (2 * p + 2) * LANES] = total.astype(jnp.bfloat16)
+    rows = made.shape[1]
+    for g in range(groups):
+        arriving[g].wait()
+        start = spill_row_of(0)
+        spill = dot(select_ref[...], held[g, :, start : start + MAIN, :].reshape(size, LANES)).astype(jnp.bfloat16)
+        for p in range(GROUP // 2):
+            main, extra = [], []
+            for b in (2 * p, 2 * p + 1):
+                start = row_of(b)
+                main.append(held[g, :, start : start + MAIN, :].reshape(size, LANES))
+                extra.append(spill[b * 64 : (b + 1) * 64])
+            total = dot(mix_ref[...], jnp.concatenate(main, axis=1))
+            total = total + dot(mix_spill_ref[...], jnp.concatenate(extra, axis=1))
+            total = total[2 * rows :] + total[rows : 2 * rows] + total[:rows]
+            made[g, :, 2 * p * LANES : (2 * p + 2) * LANES] = total.astype(jnp.bfloat16)
+        at = pl.ds((first + g) * GROUP * LANES, GROUP * LANES)
+        leaving.append(pltpu.make_async_copy(made.at[g], out_ref.at[:, at], sems.at[groups + g]))
+        leaving[-1].start()
+    for copy in leaving:
+        copy.wait()
 
 
 def combine(mix, mix_spill, select, returned, width, first, earlier):
-    step = GROUP * LANES
-    whole = pl.BlockSpec(memory_space=pltpu.VMEM)
-    return pl.pallas_call(
-        combine_kernel,
-        grid=(returned.shape[1] // (GROUP * CAP),),
-        in_specs=[whole] * 3
-        + [pl.BlockSpec((EXPERTS, GROUP * CAP, LANES), lambda g: (0, g, 0))]
-        + [pl.BlockSpec(memory_space=pl.ANY)] * len(earlier),
-        out_specs=pl.BlockSpec((mix.shape[0] // 3, step), lambda g: (0, first + g)),
-        out_shape=jax.ShapeDtypeStruct((mix.shape[0] // 3, width), jnp.bfloat16),
+    rows, step = mix.shape[0] // 3, GROUP * LANES
+    groups = returned.shape[1] // (GROUP * CAP)
+    whole, far = pl.BlockSpec(memory_space=pltpu.VMEM), pl.BlockSpec(memory_space=pltpu.HBM)
+    return pl.pallas_call(
+        functools.partial(combine_kernel, first),
+        in_specs=[whole] * 3 + [far] * (1 + len(earlier)),
+        out_specs=far,
+        out_shape=jax.ShapeDtypeStruct((rows, width), jnp.bfloat16),
         input_output_aliases={4: 0} if earlier else {},
-        compiler_params=pltpu.CompilerParams(vmem_limit_bytes=60 * MIB),
+        scratch_shapes=[
+            pltpu.VMEM((groups, EXPERTS, GROUP * CAP, LANES), jnp.bfloat16),
+            pltpu.VMEM((groups, rows, step), jnp.bfloat16),
+            pltpu.SemaphoreType.DMA((2 * groups,)),
+        ],
+        compiler_params=pltpu.CompilerParams(vmem_limit_bytes=12 * MIB),
     )(mix, mix_spill, select, returned, *earlier)
 
 
@@ -305,15 +335,15 @@
     weights = lax.all_gather(gate_up, "fsdp", axis=1, tiled=True)
     gathered = lax.all_gather(down[:, :, split:], "fsdp", axis=1, tiled=True)
     own = down[:, :, :split]
-    pieces, shards = [own], [me]
-    latest = {way: own for way in STEPS}
+    pieces, latest = [own], {way: own for way in STEPS}
+    shards = [me] + [(me - way * k + n) % n for k in range(1, 5) for way in STEPS if k <= STEPS[way]]
+    places = jnp.stack(shards).astype(jnp.int32)
 
     def step(k):
         for way, steps in STEPS.items():
             if k <= steps:
                 latest[way] = lax.ppermute(latest[way], "fsdp", [(j, (j + way) % n) for j in range(n)])
                 pieces.append(latest[way])
-                shards.append((me - way * k + n) % n)
 
     step(1)
     tokens = tie(tokens, pieces[1:])
@@ -322,14 +352,15 @@
     x = unpack(select, incoming)
     step(2)
     step(3)
-    weights, x, latest[1] = lax.optimization_barrier((weights, tie(x, pieces[1:]), latest[1]))
+    x, places = lax.optimization_barrier((tie(x, pieces[1:]), places))
+    weights, x, places, latest[1] = lax.optimization_barrier((weights, x, places, latest[1]))
     step(4)
     hidden = gate_up_rows(x, weights)
 
     result = []
     for part in range(2):
         if part == 0:
-            rows = first_rows(jnp.stack(shards).astype(jnp.int32), packing, hidden, pieces)
+            rows = first_rows(places, packing, hidden, pieces)
         else:
             rows = down_rows(packing, hidden, gathered)
         returned = lax.all_to_all(rows, "expert", split_axis=0, concat_axis=0, tiled=True)

time: 271 us -> 270 us (level)
  transfers between devices with their start and end apart: 12 -> 12, of which waited for: 8 -> 8; matrix products, arithmetic and copies ran while one was open for 1% -> 1% of each run, Pallas kernels for 15% -> 14%
where the time goes in v3:
time: 270 us; the launch traced here: 269 us
  waiting for transfers between devices  180 us (67%)
  Pallas kernels  41.8 us (15%)
  starting transfers between devices  29.7 us (11%)
  between operations  13.6 us (5%)
  local copies, waits for them, and re-layouts  4.75 us (2%)
    all_gather x1, waiting for transfers between devices, body(): weights = lax.all_gather(gate_up, 'fsdp', axis=1, tiled=True)  56.7 us
    all_to_all x2, waiting for transfers between devices, body(): lax.all_to_all(rows, 'expert', split_axis=0, concat_axis=0, tiled=True)  39.7 us
    all_to_all x1, waiting for transfers between devices, body(): lax.all_to_all(outgoing, 'expert', split_axis=0, concat_axis=0, tiled=True)  35.1 us
    ppermute x7, waiting for transfers between devices, step(): lax.ppermute(latest[way], 'fsdp', [(j, (j + way) % n) for j in range(n)])  28.1 us
    all_gather x1, waiting for transfers between devices, body(): gathered = lax.all_gather(down[:, :, split:], 'fsdp', axis=1, tiled=True)  18.5 us
    all_to_all x2, starting transfers between devices, body(): lax.all_to_all(rows, 'expert', split_axis=0, concat_axis=0, tiled=True)  11.9 us
    pallas_call x1, Pallas kernels, gate_up_rows(): pl.pallas_call(gate_up_kernel, in_specs=[pl.BlockSpec(memory_space=pltpu....  11 us
    ppermute x7, starting transfers between devices, step(): lax.ppermute(latest[way], 'fsdp', [(j, (j + way) % n) for j in range(n)])  10.3 us
  transfers between devices with their start and end apart: 12, of which 8 were waited for; matrix products, arithmetic and copies ran while one was open for 1% of the time, Pallas kernels for 14%

profile of v3, /device:TPU:64, one launch (start us, length us, event | category | flops | bytes accessed | tf_op | source)
XLA Modules:
  0.0 269.4 jit_solution(1429695193580129366)
XLA Ops:
  6.5 0.0 copy-start.11
  6.5 0.0 copy-start.12
  6.5 0.0 all-gather.3.cloned.1.call-start
  6.5 0.7 all-gather.3.cloned.1.call-update
  7.3 1.9 fusion
  9.2 0.0 copy-start.3
  9.2 1.9 collective-permute-start
  11.1 0.1 collective-permute-start.1
  11.2 0.0 copy-done.11
  11.2 0.7 copy.7.ids_ref
  11.9 0.0 copy-done.12
  11.9 0.7 copy.8.gates_ref
  12.6 7.5 %collective-permute-done.refs_1_ = bf16[1,96,2048]{2,1,0:T(8,128)(2,1)S(1)} collective-permute-done((bf16[1,96,2048]{2,1,0:T(8,128)(2,1)S(1)}, bf16[1,96,2048]{2,1,0:T(8,128)(2,1)S(1)}, u32[]{:S(2)}, u32[]{:S(2)}) %collective-permute-start) | collective-permute-done | bytes 393248 | tf_op jit(solution)/shard_map/ppermute | solution.py:345
  20.0 0.0 copy-start.4
  20.0 3.0 %collective-permute-done.1.refs_2_ = bf16[1,96,2048]{2,1,0:T(8,128)(2,1)S(1)} collective-permute-done((bf16[1,96,2048]{2,1,0:T(8,128)(2,1)S(1)}, bf16[1,96,2048]{2,1,0:T(8,128)(2,1)S(1)}, u32[]{:S(2)}, u32[]{:S(2)}) %collective-permute-start.1) | collective-permute-done | bytes 393248 | tf_op jit(solution)/shard_map/ppermute | solution.py:345
  23.1 0.0 copy-start.5
  23.1 6.8 %shard_map.55 = (bf16[32,576,128]{2,1,0:T(8,128)(2,1)}, bf16[144,512]{1,0:T(8,128)(2,1)}, bf16[144,64]{1,0:T(8,128)(2,1)}, bf16[512,512]{1,0:T(8,128)(2,1)}, bf16[512,512]{1,0:T(8,128)(2,1)}) custom-call(s32[48,8]{1,0:T(8,128)} %copy.7.ids_ref, f32[48,8]{1,0:T(8,128)} %copy.8.gates_ref, bf16[48,4096]{1,0:T(8,128)(2,1)} %tokens_ref), custom_call_target="tpu_custom_call" | custom-call | tf_op jit(solution)/shard_map/pallas_call | solution.py:100
  29.8 0.0 copy-done.3
  29.8 7.4 %all-to-all-start = ((bf16[32,576,128]{2,1,0:T(8,128)(2,1)}), bf16[32,576,128]{2,1,0:T(8,128)(2,1)}, u32[]{:S(2)}, u32[]{:S(2)}) async-start(bf16[32,576,128]{2,1,0:T(8,128)(2,1)} %get-tuple-element.23), calls=%async_computation | async-start | bytes 9437184 | tf_op jit(solution)/shard_map/all_to_all | solution.py:351
  37.3 0.0 all-gather.5.cloned.1.call-start
  37.3 0.7 all-gather.5.cloned.1.call-update
  38.0 0.0 copy-done.4
  38.0 3.0 %collective-permute-start.2 = (bf16[1,96,2048]{2,1,0:T(8,128)(2,1)S(1)}, bf16[1,96,2048]{2,1,0:T(8,128)(2,1)S(1)}, u32[]{:S(2)}, u32[]{:S(2)}) collective-permute-start(bf16[1,96,2048]{2,1,0:T(8,128)(2,1)S(1)} %collective-permute-done.refs_1_), channel_id=1, source_target_pairs={{0,32},{32,64},{64,96},{96,128},{128,160},{160,192},{192,224},{224... | collective-permute-start | bytes 1179656 | tf_op jit(solution)/shard_map/ppermute | solution.py:345
  41.0 0.0 copy-done.5
  41.0 0.0 collective-permute-start.3
  41.0 17.6 %collective-permute-done.2.refs_3_ = bf16[1,96,2048]{2,1,0:T(8,128)(2,1)S(1)} collective-permute-done((bf16[1,96,2048]{2,1,0:T(8,128)(2,1)S(1)}, bf16[1,96,2048]{2,1,0:T(8,128)(2,1)S(1)}, u32[]{:S(2)}, u32[]{:S(2)}) %collective-permute-start.2) | collective-permute-done | bytes 393248 | tf_op jit(solution)/shard_map/ppermute | solution.py:345
  58.7 0.0 copy-start.6
  58.7 2.5 collective-permute-start.4
  61.2 0.0 collective-permute-done.3.refs_4_
  61.2 0.0 copy-start.7
  61.2 0.0 collective-permute-start.5
  61.2 0.7 stack.35.places_ref
  61.9 35.1 %all-to-all-done.in_ref = bf16[32,576,128]{2,1,0:T(8,128)(2,1)} async-done(((bf16[32,576,128]{2,1,0:T(8,128)(2,1)}), bf16[32,576,128]{2,1,0:T(8,128)(2,1)}, u32[]{:S(2)}, u32[]{:S(2)}) %all-to-all-start) | async-done | bytes 4718624 | tf_op jit(solution)/shard_map/all_to_all | solution.py:351
  97.0 6.2 %shard_map.56.x_ref = bf16[576,4096]{1,0:T(8,128)(2,1)} custom-call(bf16[512,512]{1,0:T(8,128)(2,1)} %get-tuple-element.21.select_ref, bf16[32,576,128]{2,1,0:T(8,128)(2,1)} %all-to-all-done.in_ref), custom_call_target="tpu_custom_call" | custom-call | tf_op jit(solution)/shard_map/pallas_call | solution.py:126
  103.2 0.0 copy-done.6
  103.2 0.0 copy-done.7
  103.2 0.0 collective-permute-done.4.refs_5_
  103.2 0.0 copy-start.8
  103.2 0.0 collective-permute-done.5.refs_6_
  103.2 0.0 copy-start.9
  103.2 56.7 %all-gather.3.cloned.1.call-done.weights_ref = bf16[1,4096,1536]{2,1,0:T(8,128)(2,1)} async-done(((bf16[1,512,1536]{2,1,0:T(8,128)(2,1)}), bf16[1,4096,1536]{2,1,0:T(8,128)(2,1)}) %all-gather.3.cloned.1.call-update) | async-done | bytes 12582928 | tf_op jit(solution)/shard_map/all_gather | solution.py:335
  160.0 2.8 %collective-permute-start.6 = (bf16[1,96,2048]{2,1,0:T(8,128)(2,1)S(1)}, bf16[1,96,2048]{2,1,0:T(8,128)(2,1)S(1)}, u32[]{:S(2)}, u32[]{:S(2)}) collective-permute-start(bf16[1,96,2048]{2,1,0:T(8,128)(2,1)S(1)} %collective-permute-done.4.refs_5_), channel_id=1, source_target_pairs={{0,32},{32,64},{64,96},{96,128},{128,160},{160,192},{192,224},{224... | collective-permute-start | bytes 1179656 | tf_op jit(solution)/shard_map/ppermute | solution.py:345
  162.7 11.0 %shard_map.57.hidden_ref = bf16[576,768]{1,0:T(8,128)(2,1)} custom-call(bf16[576,4096]{1,0:T(8,128)(2,1)} %shard_map.56.x_ref, bf16[1,4096,1536]{2,1,0:T(8,128)(2,1)} %all-gather.3.cloned.1.call-done.weights_ref), custom_call_target="tpu_custom_call" | custom-call | tf_op jit(solution)/shard_map/pallas_call | solution.py:179
  173.7 0.0 copy-done.8
  173.7 0.0 copy-done.9
  173.7 0.0 collective-permute-done.6.refs_7_
  173.7 0.0 copy-start.10
  173.7 0.7 copy-done.10
  174.5 6.5 %shard_map.59 = bf16[32,288,128]{2,1,0:T(8,128)(2,1)} custom-call(s32[8]{0:T(128)} %stack.35.places_ref, bf16[512,512]{1,0:T(8,128)(2,1)} %get-tuple-element.22.select_ref, bf16[576,768]{1,0:T(8,128)(2,1)} %shard_map.57.hidden_ref, bf16[1,96,2048]{2,1,0:T(8,128)(2,1)} %copy-done.3, bf16[1,96,2048]{2,1,0:T(8,128)(2,1)} %copy-done.4, ...), custom_call_target="tpu_custom_call" | custom-call | tf_op jit(solution)/shard_map/pallas_call | solution.py:233
  181.0 7.1 %all-to-all-start.2 = ((bf16[32,288,128]{2,1,0:T(8,128)(2,1)}), bf16[32,288,128]{2,1,0:T(8,128)(2,1)S(1)}, u32[]{:S(2)}, u32[]{:S(2)}) async-start(bf16[32,288,128]{2,1,0:T(8,128)(2,1)} %shard_map.59), calls=%async_computation.2 | async-start | bytes 4718592 | tf_op jit(solution)/shard_map/all_to_all | solution.py:366
  188.1 18.5 %all-gather.5.cloned.1.call-done.weights_ref = bf16[1,768,2048]{2,1,0:T(8,128)(2,1)} async-done(((bf16[1,96,2048]{2,1,0:T(8,128)(2,1)}), bf16[1,768,2048]{2,1,0:T(8,128)(2,1)}) %all-gather.5.cloned.1.call-update) | async-done | bytes 3145744 | tf_op jit(solution)/shard_map/all_gather | solution.py:336
  206.5 5.6 %shard_map.58 = bf16[32,288,128]{2,1,0:T(8,128)(2,1)} custom-call(bf16[512,512]{1,0:T(8,128)(2,1)} %get-tuple-element.22.select_ref, bf16[576,768]{1,0:T(8,128)(2,1)} %shard_map.57.hidden_ref, bf16[1,768,2048]{2,1,0:T(8,128)(2,1)} %all-gather.5.cloned.1.call-done.weights_ref), custom_call_target="tpu_custom_call" | custom-call | tf_op jit(solution)/shard_map/pallas_call | solution.py:261
  212.1 0.0 copy-start
  212.1 0.0 copy-start.1
  212.1 0.0 copy-start.2
  212.1 9.0 %all-to-all-done.2.in_ref = bf16[32,288,128]{2,1,0:T(8,128)(2,1)S(1)} async-done(((bf16[32,288,128]{2,1,0:T(8,128)(2,1)}), bf16[32,288,128]{2,1,0:T(8,128)(2,1)S(1)}, u32[]{:S(2)}, u32[]{:S(2)}) %all-to-all-start.2) | async-done | bytes 2359328 | tf_op jit(solution)/shard_map/all_to_all | solution.py:366
  221.2 4.8 %all-to-all-start.1 = ((bf16[32,288,128]{2,1,0:T(8,128)(2,1)}), bf16[32,288,128]{2,1,0:T(8,128)(2,1)}, u32[]{:S(2)}, u32[]{:S(2)}) async-start(bf16[32,288,128]{2,1,0:T(8,128)(2,1)} %shard_map.58), calls=%async_computation.1 | async-start | bytes 4718592 | tf_op jit(solution)/shard_map/all_to_all | solution.py:366
  226.0 0.0 copy-done
  226.0 0.0 copy-done.1
  226.0 0.0 copy-done.2
  226.0 2.4 shard_map.60.refs_0_
  228.4 30.7 %all-to-all-done.1.in_ref = bf16[32,288,128]{2,1,0:T(8,128)(2,1)} async-done(((bf16[32,288,128]{2,1,0:T(8,128)(2,1)}), bf16[32,288,128]{2,1,0:T(8,128)(2,1)}, u32[]{:S(2)}, u32[]{:S(2)}) %all-to-all-start.1) | async-done | bytes 2359328 | tf_op jit(solution)/shard_map/all_to_all | solution.py:366
  259.1 3.5 %shard_map.61 = bf16[48,4096]{1,0:T(8,128)(2,1)} custom-call(bf16[144,512]{1,0:T(8,128)(2,1)S(1)} %copy-done.1, bf16[144,64]{1,0:T(8,128)(2,1)S(1)} %copy-done.2, bf16[512,512]{1,0:T(8,128)(2,1)S(1)} %copy-done, bf16[32,288,128]{2,1,0:T(8,128)(2,1)} %all-to-all-done.1.in_ref, bf16[48,4096]{1,0:T(8,128)(2,1)} %shard_map.60.refs_0_), custom_call_target="tpu_custom_call", output_to_operand_aliasing={{}: (4, {})} | custom-call | tf_op jit(solution)/shard_map/pallas_call | solution.py:310
Async XLA Ops:
  6.5 4.7 %copy-start.11 = (s32[48,8]{0,1:T(8,128)S(1)}, s32[48,8]{0,1:T(8,128)}, u32[]{:S(2)}) copy-start(s32[48,8]{0,1:T(8,128)} %param.6) | copy-start | bytes 4612
  6.5 5.4 %copy-start.12 = (f32[48,8]{0,1:T(8,128)S(1)}, f32[48,8]{0,1:T(8,128)}, u32[]{:S(2)}) copy-start(f32[48,8]{0,1:T(8,128)} %param.7) | copy-start | bytes 4612
  6.5 153.4 %all-gather.3.cloned.1.call-start = ((), (), s32[]{:S(2)}) async-start(), calls=%async_computation.3 | async-start | bytes 14155776 | tf_op jit(solution)/shard_map/all_gather | solution.py:335
  9.2 20.6 %copy-start.3 = (bf16[1,96,2048]{2,1,0:T(8,128)(2,1)}, bf16[1,96,2048]{2,1,0:T(8,128)(2,1)S(1)}, u32[]{:S(2)}) copy-start(bf16[1,96,2048]{2,1,0:T(8,128)(2,1)S(1)} %get-tuple-element.32.refs_0_) | copy-start | bytes 1179652
  9.2 10.9 %collective-permute-start = (bf16[1,96,2048]{2,1,0:T(8,128)(2,1)S(1)}, bf16[1,96,2048]{2,1,0:T(8,128)(2,1)S(1)}, u32[]{:S(2)}, u32[]{:S(2)}) collective-permute-start(bf16[1,96,2048]{2,1,0:T(8,128)(2,1)S(1)} %get-tuple-element.32.refs_0_), channel_id=1, source_target_pairs={{0,32},{32,64},{64,96},{96,128},{128,160},{160,192},{192,224},{224... | collective-permute-start | bytes 1179656 | tf_op jit(solution)/shard_map/ppermute | solution.py:345
  11.1 12.0 %collective-permute-start.1 = (bf16[1,96,2048]{2,1,0:T(8,128)(2,1)S(1)}, bf16[1,96,2048]{2,1,0:T(8,128)(2,1)S(1)}, u32[]{:S(2)}, u32[]{:S(2)}) collective-permute-start(bf16[1,96,2048]{2,1,0:T(8,128)(2,1)S(1)} %get-tuple-element.32.refs_0_), channel_id=1, source_target_pairs={{0,224},{32,0},{64,32},{96,64},{128,96},{160,128},{192,160},{224,1... | collective-permute-start | bytes 1179656 | tf_op jit(solution)/shard_map/ppermute | solution.py:345
  20.0 18.0 %copy-start.4 = (bf16[1,96,2048]{2,1,0:T(8,128)(2,1)}, bf16[1,96,2048]{2,1,0:T(8,128)(2,1)S(1)}, u32[]{:S(2)}) copy-start(bf16[1,96,2048]{2,1,0:T(8,128)(2,1)S(1)} %collective-permute-done.refs_1_) | copy-start | bytes 1179652
  23.1 18.0 %copy-start.5 = (bf16[1,96,2048]{2,1,0:T(8,128)(2,1)}, bf16[1,96,2048]{2,1,0:T(8,128)(2,1)S(1)}, u32[]{:S(2)}) copy-start(bf16[1,96,2048]{2,1,0:T(8,128)(2,1)S(1)} %collective-permute-done.1.refs_2_) | copy-start | bytes 1179652
  29.8 67.2 %all-to-all-start = ((bf16[32,576,128]{2,1,0:T(8,128)(2,1)}), bf16[32,576,128]{2,1,0:T(8,128)(2,1)}, u32[]{:S(2)}, u32[]{:S(2)}) async-start(bf16[32,576,128]{2,1,0:T(8,128)(2,1)} %get-tuple-element.23), calls=%async_computation | async-start | bytes 9437184 | tf_op jit(solution)/shard_map/all_to_all | solution.py:351
  37.3 169.3 %all-gather.5.cloned.1.call-start = ((), (), s32[]{:S(2)}) async-start(), calls=%async_computation.4 | async-start | bytes 3538944 | tf_op jit(solution)/shard_map/all_gather | solution.py:336
  38.0 20.6 %collective-permute-start.2 = (bf16[1,96,2048]{2,1,0:T(8,128)(2,1)S(1)}, bf16[1,96,2048]{2,1,0:T(8,128)(2,1)S(1)}, u32[]{:S(2)}, u32[]{:S(2)}) collective-permute-start(bf16[1,96,2048]{2,1,0:T(8,128)(2,1)S(1)} %collective-permute-done.refs_1_), channel_id=1, source_target_pairs={{0,32},{32,64},{64,96},{96,128},{128,160},{160,192},{192,224},{224... | collective-permute-start | bytes 1179656 | tf_op jit(solution)/shard_map/ppermute | solution.py:345
  41.0 20.1 %collective-permute-start.3 = (bf16[1,96,2048]{2,1,0:T(8,128)(2,1)S(1)}, bf16[1,96,2048]{2,1,0:T(8,128)(2,1)S(1)}, u32[]{:S(2)}, u32[]{:S(2)}) collective-permute-start(bf16[1,96,2048]{2,1,0:T(8,128)(2,1)S(1)} %collective-permute-done.1.refs_2_), channel_id=1, source_target_pairs={{0,224},{32,0},{64,32},{96,64},{128,96},{160,128},{192,160},{224,1... | collective-permute-start | bytes 1179656 | tf_op jit(solution)/shard_map/ppermute | solution.py:345
  58.7 44.5 %copy-start.6 = (bf16[1,96,2048]{2,1,0:T(8,128)(2,1)}, bf16[1,96,2048]{2,1,0:T(8,128)(2,1)S(1)}, u32[]{:S(2)}) copy-start(bf16[1,96,2048]{2,1,0:T(8,128)(2,1)S(1)} %collective-permute-done.2.refs_3_) | copy-start | bytes 1179652
  58.7 44.5 %collective-permute-start.4 = (bf16[1,96,2048]{2,1,0:T(8,128)(2,1)S(1)}, bf16[1,96,2048]{2,1,0:T(8,128)(2,1)S(1)}, u32[]{:S(2)}, u32[]{:S(2)}) collective-permute-start(bf16[1,96,2048]{2,1,0:T(8,128)(2,1)S(1)} %collective-permute-done.2.refs_3_), channel_id=1, source_target_pairs={{0,32},{32,64},{64,96},{96,128},{128,160},{160,192},{192,224},{224... | collective-permute-start | bytes 1179656 | tf_op jit(solution)/shard_map/ppermute | solution.py:345
  61.2 42.0 %copy-start.7 = (bf16[1,96,2048]{2,1,0:T(8,128)(2,1)}, bf16[1,96,2048]{2,1,0:T(8,128)(2,1)S(1)}, u32[]{:S(2)}) copy-start(bf16[1,96,2048]{2,1,0:T(8,128)(2,1)S(1)} %collective-permute-done.3.refs_4_) | copy-start | bytes 1179652
  61.2 42.1 %collective-permute-start.5 = (bf16[1,96,2048]{2,1,0:T(8,128)(2,1)S(1)}, bf16[1,96,2048]{2,1,0:T(8,128)(2,1)S(1)}, u32[]{:S(2)}, u32[]{:S(2)}) collective-permute-start(bf16[1,96,2048]{2,1,0:T(8,128)(2,1)S(1)} %collective-permute-done.3.refs_4_), channel_id=1, source_target_pairs={{0,224},{32,0},{64,32},{96,64},{128,96},{160,128},{192,160},{224,1... | collective-permute-start | bytes 1179656 | tf_op jit(solution)/shard_map/ppermute | solution.py:345
  103.2 70.5 %copy-start.8 = (bf16[1,96,2048]{2,1,0:T(8,128)(2,1)}, bf16[1,96,2048]{2,1,0:T(8,128)(2,1)S(1)}, u32[]{:S(2)}) copy-start(bf16[1,96,2048]{2,1,0:T(8,128)(2,1)S(1)} %collective-permute-done.4.refs_5_) | copy-start | bytes 1179652
  103.2 70.5 %copy-start.9 = (bf16[1,96,2048]{2,1,0:T(8,128)(2,1)}, bf16[1,96,2048]{2,1,0:T(8,128)(2,1)S(1)}, u32[]{:S(2)}) copy-start(bf16[1,96,2048]{2,1,0:T(8,128)(2,1)S(1)} %collective-permute-done.5.refs_6_) | copy-start | bytes 1179652
  160.0 13.8 %collective-permute-start.6 = (bf16[1,96,2048]{2,1,0:T(8,128)(2,1)S(1)}, bf16[1,96,2048]{2,1,0:T(8,128)(2,1)S(1)}, u32[]{:S(2)}, u32[]{:S(2)}) collective-permute-start(bf16[1,96,2048]{2,1,0:T(8,128)(2,1)S(1)} %collective-permute-done.4.refs_5_), channel_id=1, source_target_pairs={{0,32},{32,64},{64,96},{96,128},{128,160},{160,192},{192,224},{224... | collective-permute-start | bytes 1179656 | tf_op jit(solution)/shard_map/ppermute | solution.py:345
  173.7 0.8 copy-start.10
  181.0 40.2 %all-to-all-start.2 = ((bf16[32,288,128]{2,1,0:T(8,128)(2,1)}), bf16[32,288,128]{2,1,0:T(8,128)(2,1)S(1)}, u32[]{:S(2)}, u32[]{:S(2)}) async-start(bf16[32,288,128]{2,1,0:T(8,128)(2,1)} %shard_map.59), calls=%async_computation.2 | async-start | bytes 4718592 | tf_op jit(solution)/shard_map/all_to_all | solution.py:366
  212.1 13.8 %copy-start = (bf16[512,512]{1,0:T(8,128)(2,1)S(1)}, bf16[512,512]{1,0:T(8,128)(2,1)}, u32[]{:S(2)}) copy-start(bf16[512,512]{1,0:T(8,128)(2,1)} %get-tuple-element.21.select_ref) | copy-start | bytes 1572868
  212.1 13.9 %copy-start.1 = (bf16[144,512]{1,0:T(8,128)(2,1)S(1)}, bf16[144,512]{1,0:T(8,128)(2,1)}, u32[]{:S(2)}) copy-start(bf16[144,512]{1,0:T(8,128)(2,1)} %get-tuple-element.19.mix_ref) | copy-start | bytes 442372
  212.1 13.9 %copy-start.2 = (bf16[144,64]{1,0:T(8,128)(2,1)S(1)}, bf16[144,64]{1,0:T(8,128)(2,1)}, u32[]{:S(2)}) copy-start(bf16[144,64]{1,0:T(8,128)(2,1)} %get-tuple-element.20.mix_spill_ref) | copy-start | bytes 55300
  221.2 37.9 %all-to-all-start.1 = ((bf16[32,288,128]{2,1,0:T(8,128)(2,1)}), bf16[32,288,128]{2,1,0:T(8,128)(2,1)}, u32[]{:S(2)}, u32[]{:S(2)}) async-start(bf16[32,288,128]{2,1,0:T(8,128)(2,1)} %shard_map.58), calls=%async_computation.1 | async-start | bytes 4718592 | tf_op jit(solution)/shard_map/all_to_all | solution.py:366
Sparse Core Ops, SparseCore 0:
  9.1 150.7 all-gather.2
  161.7 44.7 all-gather.4

commit v4 on v3

--- a/solution.py
+++ b/solution.py
@@ -273,20 +273,24 @@
 
 
 def combine_kernel(first, mix_ref, mix_spill_ref, select_ref, in_ref, *refs):
-    out_ref, held, made, sems = refs[-4:]
+    out_ref, held, made, sems, leave_sems = refs[-5:]
     groups = held.shape[0]
+    parts = [(spill_row_of(0), MAIN)] + [(row_of(b), 2 * MAIN) for b in range(0, GROUP, 2)]
     arriving, leaving = [], []
     for g in range(groups):
-        at = pl.ds(g * GROUP * CAP, GROUP * CAP)
-        arriving.append(pltpu.make_async_copy(in_ref.at[:, at], held.at[g], sems.at[g]))
-        arriving[-1].start()
+        arriving.append([])
+        for i, (start, count) in enumerate(parts):
+            source = in_ref.at[:, pl.ds(g * GROUP * CAP + start, count)]
+            arriving[g].append(pltpu.make_async_copy(source, held.at[g, :, pl.ds(start, count)], sems.at[g, i]))
+            arriving[g][-1].start()
     size = EXPERTS * MAIN
     rows = made.shape[1]
     for g in range(groups):
-        arriving[g].wait()
+        arriving[g][0].wait()
         start = spill_row_of(0)
         spill = dot(select_ref[...], held[g, :, start : start + MAIN, :].reshape(size, LANES)).astype(jnp.bfloat16)
         for p in range(GROUP // 2):
+            arriving[g][1 + p].wait()
             main, extra = [], []
             for b in (2 * p, 2 * p + 1):
                 start = row_of(b)
@@ -297,7 +301,7 @@
             total = total[2 * rows :] + total[rows : 2 * rows] + total[:rows]
             made[g, :, 2 * p * LANES : (2 * p + 2) * LANES] = total.astype(jnp.bfloat16)
         at = pl.ds((first + g) * GROUP * LANES, GROUP * LANES)
-        leaving.append(pltpu.make_async_copy(made.at[g], out_ref.at[:, at], sems.at[groups + g]))
+        leaving.append(pltpu.make_async_copy(made.at[g], out_ref.at[:, at], leave_sems.at[g]))
         leaving[-1].start()
     for copy in leaving:
         copy.wait()
@@ -316,7 +320,8 @@
         scratch_shapes=[
             pltpu.VMEM((groups, EXPERTS, GROUP * CAP, LANES), jnp.bfloat16),
             pltpu.VMEM((groups, rows, step), jnp.bfloat16),
-            pltpu.SemaphoreType.DMA((2 * groups,)),
+            pltpu.SemaphoreType.DMA((groups, 1 + GROUP // 2)),
+            pltpu.SemaphoreType.DMA((groups,)),
         ],
         compiler_params=pltpu.CompilerParams(vmem_limit_bytes=12 * MIB),
     )(mix, mix_spill, select, returned, *earlier)

time: 270 us -> 271 us (level)
  transfers between devices with their start and end apart: 12 -> 12, of which waited for: 8 -> 8; matrix products, arithmetic and copies ran while one was open for 1% -> 1% of each run, Pallas kernels for 14% -> 15%
where the time goes in v4:
time: 271 us; the launch traced here: 270 us
  waiting for transfers between devices  178 us (66%)
  Pallas kernels  44 us (16%)
  starting transfers between devices  29.7 us (11%)
  between operations  13.6 us (5%)
  local copies, waits for them, and re-layouts  4.75 us (2%)
    all_gather x1, waiting for transfers between devices, body(): weights = lax.all_gather(gate_up, 'fsdp', axis=1, tiled=True)  56.7 us
    all_to_all x2, waiting for transfers between devices, body(): lax.all_to_all(rows, 'expert', split_axis=0, concat_axis=0, tiled=True)  38.4 us
    all_to_all x1, waiting for transfers between devices, body(): lax.all_to_all(outgoing, 'expert', split_axis=0, concat_axis=0, tiled=True)  35.1 us
    ppermute x7, waiting for transfers between devices, step(): lax.ppermute(latest[way], 'fsdp', [(j, (j + way) % n) for j in range(n)])  28.1 us
    all_gather x1, waiting for transfers between devices, body(): gathered = lax.all_gather(down[:, :, split:], 'fsdp', axis=1, tiled=True)  18.5 us
    all_to_all x2, starting transfers between devices, body(): lax.all_to_all(rows, 'expert', split_axis=0, concat_axis=0, tiled=True)  11.9 us
    pallas_call x1, Pallas kernels, gate_up_rows(): pl.pallas_call(gate_up_kernel, in_specs=[pl.BlockSpec(memory_space=pltpu....  11 us
    ppermute x7, starting transfers between devices, step(): lax.ppermute(latest[way], 'fsdp', [(j, (j + way) % n) for j in range(n)])  10.3 us
  transfers between devices with their start and end apart: 12, of which 8 were waited for; matrix products, arithmetic and copies ran while one was open for 1% of the time, Pallas kernels for 15%

profile of v4, /device:TPU:64, one launch (start us, length us, event | category | flops | bytes accessed | tf_op | source)
XLA Modules:
  0.0 270.3 jit_solution(18207830291346921927)
XLA Ops:
  6.5 0.0 copy-start.11
  6.5 0.0 copy-start.12
  6.5 0.0 all-gather.3.cloned.1.call-start
  6.5 0.7 all-gather.3.cloned.1.call-update
  7.3 1.9 fusion
  9.2 0.0 copy-start.3
  9.2 1.9 collective-permute-start
  11.1 0.1 collective-permute-start.1
  11.2 0.0 copy-done.11
  11.2 0.7 copy.7.ids_ref
  11.9 0.0 copy-done.12
  11.9 0.7 copy.8.gates_ref
  12.6 7.5 %collective-permute-done.refs_1_ = bf16[1,96,2048]{2,1,0:T(8,128)(2,1)S(1)} collective-permute-done((bf16[1,96,2048]{2,1,0:T(8,128)(2,1)S(1)}, bf16[1,96,2048]{2,1,0:T(8,128)(2,1)S(1)}, u32[]{:S(2)}, u32[]{:S(2)}) %collective-permute-start) | collective-permute-done | bytes 393248 | tf_op jit(solution)/shard_map/ppermute | solution.py:350
  20.0 0.0 copy-start.4
  20.0 3.0 %collective-permute-done.1.refs_2_ = bf16[1,96,2048]{2,1,0:T(8,128)(2,1)S(1)} collective-permute-done((bf16[1,96,2048]{2,1,0:T(8,128)(2,1)S(1)}, bf16[1,96,2048]{2,1,0:T(8,128)(2,1)S(1)}, u32[]{:S(2)}, u32[]{:S(2)}) %collective-permute-start.1) | collective-permute-done | bytes 393248 | tf_op jit(solution)/shard_map/ppermute | solution.py:350
  23.1 0.0 copy-start.5
  23.1 6.8 %shard_map.55 = (bf16[32,576,128]{2,1,0:T(8,128)(2,1)}, bf16[144,512]{1,0:T(8,128)(2,1)}, bf16[144,64]{1,0:T(8,128)(2,1)}, bf16[512,512]{1,0:T(8,128)(2,1)}, bf16[512,512]{1,0:T(8,128)(2,1)}) custom-call(s32[48,8]{1,0:T(8,128)} %copy.7.ids_ref, f32[48,8]{1,0:T(8,128)} %copy.8.gates_ref, bf16[48,4096]{1,0:T(8,128)(2,1)} %tokens_ref), custom_call_target="tpu_custom_call" | custom-call | tf_op jit(solution)/shard_map/pallas_call | solution.py:100
  29.8 0.0 copy-done.3
  29.8 7.4 %all-to-all-start = ((bf16[32,576,128]{2,1,0:T(8,128)(2,1)}), bf16[32,576,128]{2,1,0:T(8,128)(2,1)}, u32[]{:S(2)}, u32[]{:S(2)}) async-start(bf16[32,576,128]{2,1,0:T(8,128)(2,1)} %get-tuple-element.23), calls=%async_computation | async-start | bytes 9437184 | tf_op jit(solution)/shard_map/all_to_all | solution.py:356
  37.3 0.0 all-gather.5.cloned.1.call-start
  37.3 0.7 all-gather.5.cloned.1.call-update
  38.0 0.0 copy-done.4
  38.0 3.0 %collective-permute-start.2 = (bf16[1,96,2048]{2,1,0:T(8,128)(2,1)S(1)}, bf16[1,96,2048]{2,1,0:T(8,128)(2,1)S(1)}, u32[]{:S(2)}, u32[]{:S(2)}) collective-permute-start(bf16[1,96,2048]{2,1,0:T(8,128)(2,1)S(1)} %collective-permute-done.refs_1_), channel_id=1, source_target_pairs={{0,32},{32,64},{64,96},{96,128},{128,160},{160,192},{192,224},{224... | collective-permute-start | bytes 1179656 | tf_op jit(solution)/shard_map/ppermute | solution.py:350
  41.0 0.0 copy-done.5
  41.0 0.0 collective-permute-start.3
  41.0 17.6 %collective-permute-done.2.refs_3_ = bf16[1,96,2048]{2,1,0:T(8,128)(2,1)S(1)} collective-permute-done((bf16[1,96,2048]{2,1,0:T(8,128)(2,1)S(1)}, bf16[1,96,2048]{2,1,0:T(8,128)(2,1)S(1)}, u32[]{:S(2)}, u32[]{:S(2)}) %collective-permute-start.2) | collective-permute-done | bytes 393248 | tf_op jit(solution)/shard_map/ppermute | solution.py:350
  58.7 0.0 copy-start.6
  58.7 2.5 collective-permute-start.4
  61.2 0.0 collective-permute-done.3.refs_4_
  61.2 0.0 copy-start.7
  61.2 0.0 collective-permute-start.5
  61.2 0.7 stack.35.places_ref
  61.9 35.1 %all-to-all-done.in_ref = bf16[32,576,128]{2,1,0:T(8,128)(2,1)} async-done(((bf16[32,576,128]{2,1,0:T(8,128)(2,1)}), bf16[32,576,128]{2,1,0:T(8,128)(2,1)}, u32[]{:S(2)}, u32[]{:S(2)}) %all-to-all-start) | async-done | bytes 4718624 | tf_op jit(solution)/shard_map/all_to_all | solution.py:356
  97.0 6.2 %shard_map.56.x_ref = bf16[576,4096]{1,0:T(8,128)(2,1)} custom-call(bf16[512,512]{1,0:T(8,128)(2,1)} %get-tuple-element.21.select_ref, bf16[32,576,128]{2,1,0:T(8,128)(2,1)} %all-to-all-done.in_ref), custom_call_target="tpu_custom_call" | custom-call | tf_op jit(solution)/shard_map/pallas_call | solution.py:126
  103.2 0.0 copy-done.6
  103.2 0.0 copy-done.7
  103.2 0.0 collective-permute-done.4.refs_5_
  103.2 0.0 copy-start.8
  103.2 0.0 collective-permute-done.5.refs_6_
  103.2 0.0 copy-start.9
  103.2 56.7 %all-gather.3.cloned.1.call-done.weights_ref = bf16[1,4096,1536]{2,1,0:T(8,128)(2,1)} async-done(((bf16[1,512,1536]{2,1,0:T(8,128)(2,1)}), bf16[1,4096,1536]{2,1,0:T(8,128)(2,1)}) %all-gather.3.cloned.1.call-update) | async-done | bytes 12582928 | tf_op jit(solution)/shard_map/all_gather | solution.py:340
  160.0 2.8 %collective-permute-start.6 = (bf16[1,96,2048]{2,1,0:T(8,128)(2,1)S(1)}, bf16[1,96,2048]{2,1,0:T(8,128)(2,1)S(1)}, u32[]{:S(2)}, u32[]{:S(2)}) collective-permute-start(bf16[1,96,2048]{2,1,0:T(8,128)(2,1)S(1)} %collective-permute-done.4.refs_5_), channel_id=1, source_target_pairs={{0,32},{32,64},{64,96},{96,128},{128,160},{160,192},{192,224},{224... | collective-permute-start | bytes 1179656 | tf_op jit(solution)/shard_map/ppermute | solution.py:350
  162.7 11.0 %shard_map.57.hidden_ref = bf16[576,768]{1,0:T(8,128)(2,1)} custom-call(bf16[576,4096]{1,0:T(8,128)(2,1)} %shard_map.56.x_ref, bf16[1,4096,1536]{2,1,0:T(8,128)(2,1)} %all-gather.3.cloned.1.call-done.weights_ref), custom_call_target="tpu_custom_call" | custom-call | tf_op jit(solution)/shard_map/pallas_call | solution.py:179
  173.7 0.0 copy-done.8
  173.7 0.0 copy-done.9
  173.7 0.0 collective-permute-done.6.refs_7_
  173.7 0.0 copy-start.10
  173.7 0.7 copy-done.10
  174.5 6.5 %shard_map.59 = bf16[32,288,128]{2,1,0:T(8,128)(2,1)} custom-call(s32[8]{0:T(128)} %stack.35.places_ref, bf16[512,512]{1,0:T(8,128)(2,1)} %get-tuple-element.22.select_ref, bf16[576,768]{1,0:T(8,128)(2,1)} %shard_map.57.hidden_ref, bf16[1,96,2048]{2,1,0:T(8,128)(2,1)} %copy-done.3, bf16[1,96,2048]{2,1,0:T(8,128)(2,1)} %copy-done.4, ...), custom_call_target="tpu_custom_call" | custom-call | tf_op jit(solution)/shard_map/pallas_call | solution.py:233
  181.0 7.1 %all-to-all-start.2 = ((bf16[32,288,128]{2,1,0:T(8,128)(2,1)}), bf16[32,288,128]{2,1,0:T(8,128)(2,1)S(1)}, u32[]{:S(2)}, u32[]{:S(2)}) async-start(bf16[32,288,128]{2,1,0:T(8,128)(2,1)} %shard_map.59), calls=%async_computation.2 | async-start | bytes 4718592 | tf_op jit(solution)/shard_map/all_to_all | solution.py:371
  188.1 18.5 %all-gather.5.cloned.1.call-done.weights_ref = bf16[1,768,2048]{2,1,0:T(8,128)(2,1)} async-done(((bf16[1,96,2048]{2,1,0:T(8,128)(2,1)}), bf16[1,768,2048]{2,1,0:T(8,128)(2,1)}) %all-gather.5.cloned.1.call-update) | async-done | bytes 3145744 | tf_op jit(solution)/shard_map/all_gather | solution.py:341
  206.5 5.6 %shard_map.58 = bf16[32,288,128]{2,1,0:T(8,128)(2,1)} custom-call(bf16[512,512]{1,0:T(8,128)(2,1)} %get-tuple-element.22.select_ref, bf16[576,768]{1,0:T(8,128)(2,1)} %shard_map.57.hidden_ref, bf16[1,768,2048]{2,1,0:T(8,128)(2,1)} %all-gather.5.cloned.1.call-done.weights_ref), custom_call_target="tpu_custom_call" | custom-call | tf_op jit(solution)/shard_map/pallas_call | solution.py:261
  212.1 0.0 copy-start
  212.1 0.0 copy-start.1
  212.1 0.0 copy-start.2
  212.1 9.0 %all-to-all-done.2.in_ref = bf16[32,288,128]{2,1,0:T(8,128)(2,1)S(1)} async-done(((bf16[32,288,128]{2,1,0:T(8,128)(2,1)}), bf16[32,288,128]{2,1,0:T(8,128)(2,1)S(1)}, u32[]{:S(2)}, u32[]{:S(2)}) %all-to-all-start.2) | async-done | bytes 2359328 | tf_op jit(solution)/shard_map/all_to_all | solution.py:371
  221.2 4.8 %all-to-all-start.1 = ((bf16[32,288,128]{2,1,0:T(8,128)(2,1)}), bf16[32,288,128]{2,1,0:T(8,128)(2,1)}, u32[]{:S(2)}, u32[]{:S(2)}) async-start(bf16[32,288,128]{2,1,0:T(8,128)(2,1)} %shard_map.58), calls=%async_computation.1 | async-start | bytes 4718592 | tf_op jit(solution)/shard_map/all_to_all | solution.py:371
  226.0 0.0 copy-done
  226.0 0.0 copy-done.1
  226.0 0.0 copy-done.2
  226.0 3.7 %shard_map.60.refs_0_ = bf16[48,4096]{1,0:T(8,128)(2,1)} custom-call(bf16[144,512]{1,0:T(8,128)(2,1)S(1)} %copy-done.1, bf16[144,64]{1,0:T(8,128)(2,1)S(1)} %copy-done.2, bf16[512,512]{1,0:T(8,128)(2,1)S(1)} %copy-done, bf16[32,288,128]{2,1,0:T(8,128)(2,1)S(1)} %all-to-all-done.2.in_ref), custom_call_target="tpu_custom_call" | custom-call | tf_op jit(solution)/shard_map/pallas_call | solution.py:314
  229.7 29.4 %all-to-all-done.1.in_ref = bf16[32,288,128]{2,1,0:T(8,128)(2,1)} async-done(((bf16[32,288,128]{2,1,0:T(8,128)(2,1)}), bf16[32,288,128]{2,1,0:T(8,128)(2,1)}, u32[]{:S(2)}, u32[]{:S(2)}) %all-to-all-start.1) | async-done | bytes 2359328 | tf_op jit(solution)/shard_map/all_to_all | solution.py:371
  259.1 4.4 %shard_map.61 = bf16[48,4096]{1,0:T(8,128)(2,1)} custom-call(bf16[144,512]{1,0:T(8,128)(2,1)S(1)} %copy-done.1, bf16[144,64]{1,0:T(8,128)(2,1)S(1)} %copy-done.2, bf16[512,512]{1,0:T(8,128)(2,1)S(1)} %copy-done, bf16[32,288,128]{2,1,0:T(8,128)(2,1)} %all-to-all-done.1.in_ref, bf16[48,4096]{1,0:T(8,128)(2,1)} %shard_map.60.refs_0_), custom_call_target="tpu_custom_call", output_to_operand_aliasing={{}: (4, {})} | custom-call | tf_op jit(solution)/shard_map/pallas_call | solution.py:314
Async XLA Ops:
  6.5 4.7 %copy-start.11 = (s32[48,8]{0,1:T(8,128)S(1)}, s32[48,8]{0,1:T(8,128)}, u32[]{:S(2)}) copy-start(s32[48,8]{0,1:T(8,128)} %param.6) | copy-start | bytes 4612
  6.5 5.4 %copy-start.12 = (f32[48,8]{0,1:T(8,128)S(1)}, f32[48,8]{0,1:T(8,128)}, u32[]{:S(2)}) copy-start(f32[48,8]{0,1:T(8,128)} %param.7) | copy-start | bytes 4612
  6.5 153.4 %all-gather.3.cloned.1.call-start = ((), (), s32[]{:S(2)}) async-start(), calls=%async_computation.3 | async-start | bytes 14155776 | tf_op jit(solution)/shard_map/all_gather | solution.py:340
  9.2 20.6 %copy-start.3 = (bf16[1,96,2048]{2,1,0:T(8,128)(2,1)}, bf16[1,96,2048]{2,1,0:T(8,128)(2,1)S(1)}, u32[]{:S(2)}) copy-start(bf16[1,96,2048]{2,1,0:T(8,128)(2,1)S(1)} %get-tuple-element.32.refs_0_) | copy-start | bytes 1179652
  9.2 10.9 %collective-permute-start = (bf16[1,96,2048]{2,1,0:T(8,128)(2,1)S(1)}, bf16[1,96,2048]{2,1,0:T(8,128)(2,1)S(1)}, u32[]{:S(2)}, u32[]{:S(2)}) collective-permute-start(bf16[1,96,2048]{2,1,0:T(8,128)(2,1)S(1)} %get-tuple-element.32.refs_0_), channel_id=1, source_target_pairs={{0,32},{32,64},{64,96},{96,128},{128,160},{160,192},{192,224},{224... | collective-permute-start | bytes 1179656 | tf_op jit(solution)/shard_map/ppermute | solution.py:350
  11.1 12.0 %collective-permute-start.1 = (bf16[1,96,2048]{2,1,0:T(8,128)(2,1)S(1)}, bf16[1,96,2048]{2,1,0:T(8,128)(2,1)S(1)}, u32[]{:S(2)}, u32[]{:S(2)}) collective-permute-start(bf16[1,96,2048]{2,1,0:T(8,128)(2,1)S(1)} %get-tuple-element.32.refs_0_), channel_id=1, source_target_pairs={{0,224},{32,0},{64,32},{96,64},{128,96},{160,128},{192,160},{224,1... | collective-permute-start | bytes 1179656 | tf_op jit(solution)/shard_map/ppermute | solution.py:350
  20.0 18.0 %copy-start.4 = (bf16[1,96,2048]{2,1,0:T(8,128)(2,1)}, bf16[1,96,2048]{2,1,0:T(8,128)(2,1)S(1)}, u32[]{:S(2)}) copy-start(bf16[1,96,2048]{2,1,0:T(8,128)(2,1)S(1)} %collective-permute-done.refs_1_) | copy-start | bytes 1179652
  23.1 18.0 %copy-start.5 = (bf16[1,96,2048]{2,1,0:T(8,128)(2,1)}, bf16[1,96,2048]{2,1,0:T(8,128)(2,1)S(1)}, u32[]{:S(2)}) copy-start(bf16[1,96,2048]{2,1,0:T(8,128)(2,1)S(1)} %collective-permute-done.1.refs_2_) | copy-start | bytes 1179652
  29.8 67.2 %all-to-all-start = ((bf16[32,576,128]{2,1,0:T(8,128)(2,1)}), bf16[32,576,128]{2,1,0:T(8,128)(2,1)}, u32[]{:S(2)}, u32[]{:S(2)}) async-start(bf16[32,576,128]{2,1,0:T(8,128)(2,1)} %get-tuple-element.23), calls=%async_computation | async-start | bytes 9437184 | tf_op jit(solution)/shard_map/all_to_all | solution.py:356
  37.3 169.3 %all-gather.5.cloned.1.call-start = ((), (), s32[]{:S(2)}) async-start(), calls=%async_computation.4 | async-start | bytes 3538944 | tf_op jit(solution)/shard_map/all_gather | solution.py:341
  38.0 20.6 %collective-permute-start.2 = (bf16[1,96,2048]{2,1,0:T(8,128)(2,1)S(1)}, bf16[1,96,2048]{2,1,0:T(8,128)(2,1)S(1)}, u32[]{:S(2)}, u32[]{:S(2)}) collective-permute-start(bf16[1,96,2048]{2,1,0:T(8,128)(2,1)S(1)} %collective-permute-done.refs_1_), channel_id=1, source_target_pairs={{0,32},{32,64},{64,96},{96,128},{128,160},{160,192},{192,224},{224... | collective-permute-start | bytes 1179656 | tf_op jit(solution)/shard_map/ppermute | solution.py:350
  41.0 20.1 %collective-permute-start.3 = (bf16[1,96,2048]{2,1,0:T(8,128)(2,1)S(1)}, bf16[1,96,2048]{2,1,0:T(8,128)(2,1)S(1)}, u32[]{:S(2)}, u32[]{:S(2)}) collective-permute-start(bf16[1,96,2048]{2,1,0:T(8,128)(2,1)S(1)} %collective-permute-done.1.refs_2_), channel_id=1, source_target_pairs={{0,224},{32,0},{64,32},{96,64},{128,96},{160,128},{192,160},{224,1... | collective-permute-start | bytes 1179656 | tf_op jit(solution)/shard_map/ppermute | solution.py:350
  58.7 44.5 %copy-start.6 = (bf16[1,96,2048]{2,1,0:T(8,128)(2,1)}, bf16[1,96,2048]{2,1,0:T(8,128)(2,1)S(1)}, u32[]{:S(2)}) copy-start(bf16[1,96,2048]{2,1,0:T(8,128)(2,1)S(1)} %collective-permute-done.2.refs_3_) | copy-start | bytes 1179652
  58.7 44.5 %collective-permute-start.4 = (bf16[1,96,2048]{2,1,0:T(8,128)(2,1)S(1)}, bf16[1,96,2048]{2,1,0:T(8,128)(2,1)S(1)}, u32[]{:S(2)}, u32[]{:S(2)}) collective-permute-start(bf16[1,96,2048]{2,1,0:T(8,128)(2,1)S(1)} %collective-permute-done.2.refs_3_), channel_id=1, source_target_pairs={{0,32},{32,64},{64,96},{96,128},{128,160},{160,192},{192,224},{224... | collective-permute-start | bytes 1179656 | tf_op jit(solution)/shard_map/ppermute | solution.py:350
  61.2 42.0 %copy-start.7 = (bf16[1,96,2048]{2,1,0:T(8,128)(2,1)}, bf16[1,96,2048]{2,1,0:T(8,128)(2,1)S(1)}, u32[]{:S(2)}) copy-start(bf16[1,96,2048]{2,1,0:T(8,128)(2,1)S(1)} %collective-permute-done.3.refs_4_) | copy-start | bytes 1179652
  61.2 42.1 %collective-permute-start.5 = (bf16[1,96,2048]{2,1,0:T(8,128)(2,1)S(1)}, bf16[1,96,2048]{2,1,0:T(8,128)(2,1)S(1)}, u32[]{:S(2)}, u32[]{:S(2)}) collective-permute-start(bf16[1,96,2048]{2,1,0:T(8,128)(2,1)S(1)} %collective-permute-done.3.refs_4_), channel_id=1, source_target_pairs={{0,224},{32,0},{64,32},{96,64},{128,96},{160,128},{192,160},{224,1... | collective-permute-start | bytes 1179656 | tf_op jit(solution)/shard_map/ppermute | solution.py:350
  103.2 70.5 %copy-start.8 = (bf16[1,96,2048]{2,1,0:T(8,128)(2,1)}, bf16[1,96,2048]{2,1,0:T(8,128)(2,1)S(1)}, u32[]{:S(2)}) copy-start(bf16[1,96,2048]{2,1,0:T(8,128)(2,1)S(1)} %collective-permute-done.4.refs_5_) | copy-start | bytes 1179652
  103.2 70.5 %copy-start.9 = (bf16[1,96,2048]{2,1,0:T(8,128)(2,1)}, bf16[1,96,2048]{2,1,0:T(8,128)(2,1)S(1)}, u32[]{:S(2)}) copy-start(bf16[1,96,2048]{2,1,0:T(8,128)(2,1)S(1)} %collective-permute-done.5.refs_6_) | copy-start | bytes 1179652
  160.0 13.8 %collective-permute-start.6 = (bf16[1,96,2048]{2,1,0:T(8,128)(2,1)S(1)}, bf16[1,96,2048]{2,1,0:T(8,128)(2,1)S(1)}, u32[]{:S(2)}, u32[]{:S(2)}) collective-permute-start(bf16[1,96,2048]{2,1,0:T(8,128)(2,1)S(1)} %collective-permute-done.4.refs_5_), channel_id=1, source_target_pairs={{0,32},{32,64},{64,96},{96,128},{128,160},{160,192},{192,224},{224... | collective-permute-start | bytes 1179656 | tf_op jit(solution)/shard_map/ppermute | solution.py:350
  173.7 0.8 copy-start.10
  181.0 40.2 %all-to-all-start.2 = ((bf16[32,288,128]{2,1,0:T(8,128)(2,1)}), bf16[32,288,128]{2,1,0:T(8,128)(2,1)S(1)}, u32[]{:S(2)}, u32[]{:S(2)}) async-start(bf16[32,288,128]{2,1,0:T(8,128)(2,1)} %shard_map.59), calls=%async_computation.2 | async-start | bytes 4718592 | tf_op jit(solution)/shard_map/all_to_all | solution.py:371
  212.1 13.8 %copy-start = (bf16[512,512]{1,0:T(8,128)(2,1)S(1)}, bf16[512,512]{1,0:T(8,128)(2,1)}, u32[]{:S(2)}) copy-start(bf16[512,512]{1,0:T(8,128)(2,1)} %get-tuple-element.21.select_ref) | copy-start | bytes 1572868
  212.1 13.9 %copy-start.1 = (bf16[144,512]{1,0:T(8,128)(2,1)S(1)}, bf16[144,512]{1,0:T(8,128)(2,1)}, u32[]{:S(2)}) copy-start(bf16[144,512]{1,0:T(8,128)(2,1)} %get-tuple-element.19.mix_ref) | copy-start | bytes 442372
  212.1 13.9 %copy-start.2 = (bf16[144,64]{1,0:T(8,128)(2,1)S(1)}, bf16[144,64]{1,0:T(8,128)(2,1)}, u32[]{:S(2)}) copy-start(bf16[144,64]{1,0:T(8,128)(2,1)} %get-tuple-element.20.mix_spill_ref) | copy-start | bytes 55300
  221.2 37.9 %all-to-all-start.1 = ((bf16[32,288,128]{2,1,0:T(8,128)(2,1)}), bf16[32,288,128]{2,1,0:T(8,128)(2,1)}, u32[]{:S(2)}, u32[]{:S(2)}) async-start(bf16[32,288,128]{2,1,0:T(8,128)(2,1)} %shard_map.58), calls=%async_computation.1 | async-start | bytes 4718592 | tf_op jit(solution)/shard_map/all_to_all | solution.py:371
Sparse Core Ops, SparseCore 0:
  9.1 150.7 all-gather.2
  161.7 44.7 all-gather.4

commit v5 on v3

--- a/solution.py
+++ b/solution.py
@@ -274,30 +274,28 @@
 
 def combine_kernel(first, mix_ref, mix_spill_ref, select_ref, in_ref, *refs):
     out_ref, held, made, sems = refs[-4:]
-    groups = held.shape[0]
-    arriving, leaving = [], []
-    for g in range(groups):
-        at = pl.ds(g * GROUP * CAP, GROUP * CAP)
-        arriving.append(pltpu.make_async_copy(in_ref.at[:, at], held.at[g], sems.at[g]))
-        arriving[-1].start()
+    groups = made.shape[0]
+    leaving = []
+    arriving = pltpu.make_async_copy(in_ref, held, sems.at[groups])
+    arriving.start()
+    arriving.wait()
     size = EXPERTS * MAIN
     rows = made.shape[1]
     for g in range(groups):
-        arriving[g].wait()
-        start = spill_row_of(0)
-        spill = dot(select_ref[...], held[g, :, start : start + MAIN, :].reshape(size, LANES)).astype(jnp.bfloat16)
+        start = spill_row_of(g)
+        spill = dot(select_ref[...], held[:, start : start + MAIN, :].reshape(size, LANES)).astype(jnp.bfloat16)
         for p in range(GROUP // 2):
             main, extra = [], []
             for b in (2 * p, 2 * p + 1):
-                start = row_of(b)
-                main.append(held[g, :, start : start + MAIN, :].reshape(size, LANES))
+                start = row_of(g * GROUP + b)
+                main.append(held[:, start : start + MAIN, :].reshape(size, LANES))
                 extra.append(spill[b * 64 : (b + 1) * 64])
             total = dot(mix_ref[...], jnp.concatenate(main, axis=1))
             total = total + dot(mix_spill_ref[...], jnp.concatenate(extra, axis=1))
             total = total[2 * rows :] + total[rows : 2 * rows] + total[:rows]
             made[g, :, 2 * p * LANES : (2 * p + 2) * LANES] = total.astype(jnp.bfloat16)
         at = pl.ds((first + g) * GROUP * LANES, GROUP * LANES)
-        leaving.append(pltpu.make_async_copy(made.at[g], out_ref.at[:, at], sems.at[groups + g]))
+        leaving.append(pltpu.make_async_copy(made.at[g], out_ref.at[:, at], sems.at[g]))
         leaving[-1].start()
     for copy in leaving:
         copy.wait()
@@ -314,9 +312,9 @@
         out_shape=jax.ShapeDtypeStruct((rows, width), jnp.bfloat16),
         input_output_aliases={4: 0} if earlier else {},
         scratch_shapes=[
-            pltpu.VMEM((groups, EXPERTS, GROUP * CAP, LANES), jnp.bfloat16),
+            pltpu.VMEM(returned.shape, jnp.bfloat16),
             pltpu.VMEM((groups, rows, step), jnp.bfloat16),
-            pltpu.SemaphoreType.DMA((2 * groups,)),
+            pltpu.SemaphoreType.DMA((groups + 1,)),
         ],
         compiler_params=pltpu.CompilerParams(vmem_limit_bytes=12 * MIB),
     )(mix, mix_spill, select, returned, *earlier)

time: 270 us -> 270 us (level)
  no operation moved by 1% of the time
where the time goes in v5:
time: 270 us
  waiting for transfers between devices  180 us (67%)
  Pallas kernels  41.9 us (16%)
  starting transfers between devices  29.7 us (11%)
  between operations  13.6 us (5%)
  local copies, waits for them, and re-layouts  4.75 us (2%)
    all_gather x1, waiting for transfers between devices, body(): weights = lax.all_gather(gate_up, 'fsdp', axis=1, tiled=True)  56.7 us
    all_to_all x2, waiting for transfers between devices, body(): lax.all_to_all(rows, 'expert', split_axis=0, concat_axis=0, tiled=True)  39.8 us
    all_to_all x1, waiting for transfers between devices, body(): lax.all_to_all(outgoing, 'expert', split_axis=0, concat_axis=0, tiled=True)  35.1 us
    ppermute x7, waiting for transfers between devices, step(): lax.ppermute(latest[way], 'fsdp', [(j, (j + way) % n) for j in range(n)])  28.1 us
    all_gather x1, waiting for transfers between devices, body(): gathered = lax.all_gather(down[:, :, split:], 'fsdp', axis=1, tiled=True)  18.5 us
    all_to_all x2, starting transfers between devices, body(): lax.all_to_all(rows, 'expert', split_axis=0, concat_axis=0, tiled=True)  11.9 us
    pallas_call x1, Pallas kernels, gate_up_rows(): pl.pallas_call(gate_up_kernel, in_specs=[pl.BlockSpec(memory_space=pltpu....  11 us
    ppermute x7, starting transfers between devices, step(): lax.ppermute(latest[way], 'fsdp', [(j, (j + way) % n) for j in range(n)])  10.3 us
  transfers between devices with their start and end apart: 12, of which 8 were waited for; matrix products, arithmetic and copies ran while one was open for 1% of the time, Pallas kernels for 14%

profile of v5, /device:TPU:64, one launch (start us, length us, event | category | flops | bytes accessed | tf_op | source)
XLA Modules:
  0.0 269.6 jit_solution(16839861945638325073)
XLA Ops:
  6.5 0.0 copy-start.11
  6.5 0.0 copy-start.12
  6.5 0.0 all-gather.3.cloned.1.call-start
  6.5 0.7 all-gather.3.cloned.1.call-update
  7.3 1.9 fusion
  9.2 0.0 copy-start.3
  9.2 1.9 collective-permute-start
  11.1 0.1 collective-permute-start.1
  11.2 0.0 copy-done.11
  11.2 0.7 copy.7.ids_ref
  11.9 0.0 copy-done.12
  11.9 0.7 copy.8.gates_ref
  12.6 7.5 %collective-permute-done.refs_1_ = bf16[1,96,2048]{2,1,0:T(8,128)(2,1)S(1)} collective-permute-done((bf16[1,96,2048]{2,1,0:T(8,128)(2,1)S(1)}, bf16[1,96,2048]{2,1,0:T(8,128)(2,1)S(1)}, u32[]{:S(2)}, u32[]{:S(2)}) %collective-permute-start) | collective-permute-done | bytes 393248 | tf_op jit(solution)/shard_map/ppermute | solution.py:343
  20.0 0.0 copy-start.4
  20.0 3.0 %collective-permute-done.1.refs_2_ = bf16[1,96,2048]{2,1,0:T(8,128)(2,1)S(1)} collective-permute-done((bf16[1,96,2048]{2,1,0:T(8,128)(2,1)S(1)}, bf16[1,96,2048]{2,1,0:T(8,128)(2,1)S(1)}, u32[]{:S(2)}, u32[]{:S(2)}) %collective-permute-start.1) | collective-permute-done | bytes 393248 | tf_op jit(solution)/shard_map/ppermute | solution.py:343
  23.1 0.0 copy-start.5
  23.1 6.8 %shard_map.55 = (bf16[32,576,128]{2,1,0:T(8,128)(2,1)}, bf16[144,512]{1,0:T(8,128)(2,1)}, bf16[144,64]{1,0:T(8,128)(2,1)}, bf16[512,512]{1,0:T(8,128)(2,1)}, bf16[512,512]{1,0:T(8,128)(2,1)}) custom-call(s32[48,8]{1,0:T(8,128)} %copy.7.ids_ref, f32[48,8]{1,0:T(8,128)} %copy.8.gates_ref, bf16[48,4096]{1,0:T(8,128)(2,1)} %tokens_ref), custom_call_target="tpu_custom_call" | custom-call | tf_op jit(solution)/shard_map/pallas_call | solution.py:100
  29.8 0.0 copy-done.3
  29.8 7.4 %all-to-all-start = ((bf16[32,576,128]{2,1,0:T(8,128)(2,1)}), bf16[32,576,128]{2,1,0:T(8,128)(2,1)}, u32[]{:S(2)}, u32[]{:S(2)}) async-start(bf16[32,576,128]{2,1,0:T(8,128)(2,1)} %get-tuple-element.23), calls=%async_computation | async-start | bytes 9437184 | tf_op jit(solution)/shard_map/all_to_all | solution.py:349
  37.3 0.0 all-gather.5.cloned.1.call-start
  37.3 0.7 all-gather.5.cloned.1.call-update
  38.0 0.0 copy-done.4
  38.0 3.0 %collective-permute-start.2 = (bf16[1,96,2048]{2,1,0:T(8,128)(2,1)S(1)}, bf16[1,96,2048]{2,1,0:T(8,128)(2,1)S(1)}, u32[]{:S(2)}, u32[]{:S(2)}) collective-permute-start(bf16[1,96,2048]{2,1,0:T(8,128)(2,1)S(1)} %collective-permute-done.refs_1_), channel_id=1, source_target_pairs={{0,32},{32,64},{64,96},{96,128},{128,160},{160,192},{192,224},{224... | collective-permute-start | bytes 1179656 | tf_op jit(solution)/shard_map/ppermute | solution.py:343
  41.0 0.0 copy-done.5
  41.0 0.0 collective-permute-start.3
  41.0 17.6 %collective-permute-done.2.refs_3_ = bf16[1,96,2048]{2,1,0:T(8,128)(2,1)S(1)} collective-permute-done((bf16[1,96,2048]{2,1,0:T(8,128)(2,1)S(1)}, bf16[1,96,2048]{2,1,0:T(8,128)(2,1)S(1)}, u32[]{:S(2)}, u32[]{:S(2)}) %collective-permute-start.2) | collective-permute-done | bytes 393248 | tf_op jit(solution)/shard_map/ppermute | solution.py:343
  58.7 0.0 copy-start.6
  58.7 2.5 collective-permute-start.4
  61.2 0.0 collective-permute-done.3.refs_4_
  61.2 0.0 copy-start.7
  61.2 0.0 collective-permute-start.5
  61.2 0.7 stack.35.places_ref
  61.9 35.1 %all-to-all-done.in_ref = bf16[32,576,128]{2,1,0:T(8,128)(2,1)} async-done(((bf16[32,576,128]{2,1,0:T(8,128)(2,1)}), bf16[32,576,128]{2,1,0:T(8,128)(2,1)}, u32[]{:S(2)}, u32[]{:S(2)}) %all-to-all-start) | async-done | bytes 4718624 | tf_op jit(solution)/shard_map/all_to_all | solution.py:349
  97.0 6.2 %shard_map.56.x_ref = bf16[576,4096]{1,0:T(8,128)(2,1)} custom-call(bf16[512,512]{1,0:T(8,128)(2,1)} %get-tuple-element.21.select_ref, bf16[32,576,128]{2,1,0:T(8,128)(2,1)} %all-to-all-done.in_ref), custom_call_target="tpu_custom_call" | custom-call | tf_op jit(solution)/shard_map/pallas_call | solution.py:126
  103.2 0.0 copy-done.6
  103.2 0.0 copy-done.7
  103.2 0.0 collective-permute-done.4.refs_5_
  103.2 0.0 copy-start.8
  103.2 0.0 collective-permute-done.5.refs_6_
  103.2 0.0 copy-start.9
  103.2 56.7 %all-gather.3.cloned.1.call-done.weights_ref = bf16[1,4096,1536]{2,1,0:T(8,128)(2,1)} async-done(((bf16[1,512,1536]{2,1,0:T(8,128)(2,1)}), bf16[1,4096,1536]{2,1,0:T(8,128)(2,1)}) %all-gather.3.cloned.1.call-update) | async-done | bytes 12582928 | tf_op jit(solution)/shard_map/all_gather | solution.py:333
  160.0 2.8 %collective-permute-start.6 = (bf16[1,96,2048]{2,1,0:T(8,128)(2,1)S(1)}, bf16[1,96,2048]{2,1,0:T(8,128)(2,1)S(1)}, u32[]{:S(2)}, u32[]{:S(2)}) collective-permute-start(bf16[1,96,2048]{2,1,0:T(8,128)(2,1)S(1)} %collective-permute-done.4.refs_5_), channel_id=1, source_target_pairs={{0,32},{32,64},{64,96},{96,128},{128,160},{160,192},{192,224},{224... | collective-permute-start | bytes 1179656 | tf_op jit(solution)/shard_map/ppermute | solution.py:343
  162.7 11.0 %shard_map.57.hidden_ref = bf16[576,768]{1,0:T(8,128)(2,1)} custom-call(bf16[576,4096]{1,0:T(8,128)(2,1)} %shard_map.56.x_ref, bf16[1,4096,1536]{2,1,0:T(8,128)(2,1)} %all-gather.3.cloned.1.call-done.weights_ref), custom_call_target="tpu_custom_call" | custom-call | tf_op jit(solution)/shard_map/pallas_call | solution.py:179
  173.7 0.0 copy-done.8
  173.7 0.0 copy-done.9
  173.7 0.0 collective-permute-done.6.refs_7_
  173.7 0.0 copy-start.10
  173.7 0.7 copy-done.10
  174.5 6.5 %shard_map.59 = bf16[32,288,128]{2,1,0:T(8,128)(2,1)} custom-call(s32[8]{0:T(128)} %stack.35.places_ref, bf16[512,512]{1,0:T(8,128)(2,1)} %get-tuple-element.22.select_ref, bf16[576,768]{1,0:T(8,128)(2,1)} %shard_map.57.hidden_ref, bf16[1,96,2048]{2,1,0:T(8,128)(2,1)} %copy-done.3, bf16[1,96,2048]{2,1,0:T(8,128)(2,1)} %copy-done.4, ...), custom_call_target="tpu_custom_call" | custom-call | tf_op jit(solution)/shard_map/pallas_call | solution.py:233
  181.0 7.1 %all-to-all-start.2 = ((bf16[32,288,128]{2,1,0:T(8,128)(2,1)}), bf16[32,288,128]{2,1,0:T(8,128)(2,1)S(1)}, u32[]{:S(2)}, u32[]{:S(2)}) async-start(bf16[32,288,128]{2,1,0:T(8,128)(2,1)} %shard_map.59), calls=%async_computation.2 | async-start | bytes 4718592 | tf_op jit(solution)/shard_map/all_to_all | solution.py:364
  188.1 18.5 %all-gather.5.cloned.1.call-done.weights_ref = bf16[1,768,2048]{2,1,0:T(8,128)(2,1)} async-done(((bf16[1,96,2048]{2,1,0:T(8,128)(2,1)}), bf16[1,768,2048]{2,1,0:T(8,128)(2,1)}) %all-gather.5.cloned.1.call-update) | async-done | bytes 3145744 | tf_op jit(solution)/shard_map/all_gather | solution.py:334
  206.5 5.6 %shard_map.58 = bf16[32,288,128]{2,1,0:T(8,128)(2,1)} custom-call(bf16[512,512]{1,0:T(8,128)(2,1)} %get-tuple-element.22.select_ref, bf16[576,768]{1,0:T(8,128)(2,1)} %shard_map.57.hidden_ref, bf16[1,768,2048]{2,1,0:T(8,128)(2,1)} %all-gather.5.cloned.1.call-done.weights_ref), custom_call_target="tpu_custom_call" | custom-call | tf_op jit(solution)/shard_map/pallas_call | solution.py:261
  212.1 0.0 copy-start
  212.1 0.0 copy-start.1
  212.1 0.0 copy-start.2
  212.1 9.0 %all-to-all-done.2.in_ref = bf16[32,288,128]{2,1,0:T(8,128)(2,1)S(1)} async-done(((bf16[32,288,128]{2,1,0:T(8,128)(2,1)}), bf16[32,288,128]{2,1,0:T(8,128)(2,1)S(1)}, u32[]{:S(2)}, u32[]{:S(2)}) %all-to-all-start.2) | async-done | bytes 2359328 | tf_op jit(solution)/shard_map/all_to_all | solution.py:364
  221.2 4.8 %all-to-all-start.1 = ((bf16[32,288,128]{2,1,0:T(8,128)(2,1)}), bf16[32,288,128]{2,1,0:T(8,128)(2,1)}, u32[]{:S(2)}, u32[]{:S(2)}) async-start(bf16[32,288,128]{2,1,0:T(8,128)(2,1)} %shard_map.58), calls=%async_computation.1 | async-start | bytes 4718592 | tf_op jit(solution)/shard_map/all_to_all | solution.py:364
  226.0 0.0 copy-done
  226.0 0.0 copy-done.1
  226.0 0.0 copy-done.2
  226.0 2.2 shard_map.60.refs_0_
  228.2 30.8 %all-to-all-done.1.in_ref = bf16[32,288,128]{2,1,0:T(8,128)(2,1)} async-done(((bf16[32,288,128]{2,1,0:T(8,128)(2,1)}), bf16[32,288,128]{2,1,0:T(8,128)(2,1)}, u32[]{:S(2)}, u32[]{:S(2)}) %all-to-all-start.1) | async-done | bytes 2359328 | tf_op jit(solution)/shard_map/all_to_all | solution.py:364
  259.1 3.7 %shard_map.61 = bf16[48,4096]{1,0:T(8,128)(2,1)} custom-call(bf16[144,512]{1,0:T(8,128)(2,1)S(1)} %copy-done.1, bf16[144,64]{1,0:T(8,128)(2,1)S(1)} %copy-done.2, bf16[512,512]{1,0:T(8,128)(2,1)S(1)} %copy-done, bf16[32,288,128]{2,1,0:T(8,128)(2,1)} %all-to-all-done.1.in_ref, bf16[48,4096]{1,0:T(8,128)(2,1)} %shard_map.60.refs_0_), custom_call_target="tpu_custom_call", output_to_operand_aliasing={{}: (4, {})} | custom-call | tf_op jit(solution)/shard_map/pallas_call | solution.py:308
Async XLA Ops:
  6.5 4.7 %copy-start.11 = (s32[48,8]{0,1:T(8,128)S(1)}, s32[48,8]{0,1:T(8,128)}, u32[]{:S(2)}) copy-start(s32[48,8]{0,1:T(8,128)} %param.6) | copy-start | bytes 4612
  6.5 5.4 %copy-start.12 = (f32[48,8]{0,1:T(8,128)S(1)}, f32[48,8]{0,1:T(8,128)}, u32[]{:S(2)}) copy-start(f32[48,8]{0,1:T(8,128)} %param.7) | copy-start | bytes 4612
  6.5 153.4 %all-gather.3.cloned.1.call-start = ((), (), s32[]{:S(2)}) async-start(), calls=%async_computation.3 | async-start | bytes 14155776 | tf_op jit(solution)/shard_map/all_gather | solution.py:333
  9.2 20.6 %copy-start.3 = (bf16[1,96,2048]{2,1,0:T(8,128)(2,1)}, bf16[1,96,2048]{2,1,0:T(8,128)(2,1)S(1)}, u32[]{:S(2)}) copy-start(bf16[1,96,2048]{2,1,0:T(8,128)(2,1)S(1)} %get-tuple-element.32.refs_0_) | copy-start | bytes 1179652
  9.2 10.9 %collective-permute-start = (bf16[1,96,2048]{2,1,0:T(8,128)(2,1)S(1)}, bf16[1,96,2048]{2,1,0:T(8,128)(2,1)S(1)}, u32[]{:S(2)}, u32[]{:S(2)}) collective-permute-start(bf16[1,96,2048]{2,1,0:T(8,128)(2,1)S(1)} %get-tuple-element.32.refs_0_), channel_id=1, source_target_pairs={{0,32},{32,64},{64,96},{96,128},{128,160},{160,192},{192,224},{224... | collective-permute-start | bytes 1179656 | tf_op jit(solution)/shard_map/ppermute | solution.py:343
  11.1 12.0 %collective-permute-start.1 = (bf16[1,96,2048]{2,1,0:T(8,128)(2,1)S(1)}, bf16[1,96,2048]{2,1,0:T(8,128)(2,1)S(1)}, u32[]{:S(2)}, u32[]{:S(2)}) collective-permute-start(bf16[1,96,2048]{2,1,0:T(8,128)(2,1)S(1)} %get-tuple-element.32.refs_0_), channel_id=1, source_target_pairs={{0,224},{32,0},{64,32},{96,64},{128,96},{160,128},{192,160},{224,1... | collective-permute-start | bytes 1179656 | tf_op jit(solution)/shard_map/ppermute | solution.py:343
  20.0 18.0 %copy-start.4 = (bf16[1,96,2048]{2,1,0:T(8,128)(2,1)}, bf16[1,96,2048]{2,1,0:T(8,128)(2,1)S(1)}, u32[]{:S(2)}) copy-start(bf16[1,96,2048]{2,1,0:T(8,128)(2,1)S(1)} %collective-permute-done.refs_1_) | copy-start | bytes 1179652
  23.1 18.0 %copy-start.5 = (bf16[1,96,2048]{2,1,0:T(8,128)(2,1)}, bf16[1,96,2048]{2,1,0:T(8,128)(2,1)S(1)}, u32[]{:S(2)}) copy-start(bf16[1,96,2048]{2,1,0:T(8,128)(2,1)S(1)} %collective-permute-done.1.refs_2_) | copy-start | bytes 1179652
  29.8 67.2 %all-to-all-start = ((bf16[32,576,128]{2,1,0:T(8,128)(2,1)}), bf16[32,576,128]{2,1,0:T(8,128)(2,1)}, u32[]{:S(2)}, u32[]{:S(2)}) async-start(bf16[32,576,128]{2,1,0:T(8,128)(2,1)} %get-tuple-element.23), calls=%async_computation | async-start | bytes 9437184 | tf_op jit(solution)/shard_map/all_to_all | solution.py:349
  37.3 169.3 %all-gather.5.cloned.1.call-start = ((), (), s32[]{:S(2)}) async-start(), calls=%async_computation.4 | async-start | bytes 3538944 | tf_op jit(solution)/shard_map/all_gather | solution.py:334
  38.0 20.6 %collective-permute-start.2 = (bf16[1,96,2048]{2,1,0:T(8,128)(2,1)S(1)}, bf16[1,96,2048]{2,1,0:T(8,128)(2,1)S(1)}, u32[]{:S(2)}, u32[]{:S(2)}) collective-permute-start(bf16[1,96,2048]{2,1,0:T(8,128)(2,1)S(1)} %collective-permute-done.refs_1_), channel_id=1, source_target_pairs={{0,32},{32,64},{64,96},{96,128},{128,160},{160,192},{192,224},{224... | collective-permute-start | bytes 1179656 | tf_op jit(solution)/shard_map/ppermute | solution.py:343
  41.0 20.1 %collective-permute-start.3 = (bf16[1,96,2048]{2,1,0:T(8,128)(2,1)S(1)}, bf16[1,96,2048]{2,1,0:T(8,128)(2,1)S(1)}, u32[]{:S(2)}, u32[]{:S(2)}) collective-permute-start(bf16[1,96,2048]{2,1,0:T(8,128)(2,1)S(1)} %collective-permute-done.1.refs_2_), channel_id=1, source_target_pairs={{0,224},{32,0},{64,32},{96,64},{128,96},{160,128},{192,160},{224,1... | collective-permute-start | bytes 1179656 | tf_op jit(solution)/shard_map/ppermute | solution.py:343
  58.7 44.5 %copy-start.6 = (bf16[1,96,2048]{2,1,0:T(8,128)(2,1)}, bf16[1,96,2048]{2,1,0:T(8,128)(2,1)S(1)}, u32[]{:S(2)}) copy-start(bf16[1,96,2048]{2,1,0:T(8,128)(2,1)S(1)} %collective-permute-done.2.refs_3_) | copy-start | bytes 1179652
  58.7 44.5 %collective-permute-start.4 = (bf16[1,96,2048]{2,1,0:T(8,128)(2,1)S(1)}, bf16[1,96,2048]{2,1,0:T(8,128)(2,1)S(1)}, u32[]{:S(2)}, u32[]{:S(2)}) collective-permute-start(bf16[1,96,2048]{2,1,0:T(8,128)(2,1)S(1)} %collective-permute-done.2.refs_3_), channel_id=1, source_target_pairs={{0,32},{32,64},{64,96},{96,128},{128,160},{160,192},{192,224},{224... | collective-permute-start | bytes 1179656 | tf_op jit(solution)/shard_map/ppermute | solution.py:343
  61.2 42.0 %copy-start.7 = (bf16[1,96,2048]{2,1,0:T(8,128)(2,1)}, bf16[1,96,2048]{2,1,0:T(8,128)(2,1)S(1)}, u32[]{:S(2)}) copy-start(bf16[1,96,2048]{2,1,0:T(8,128)(2,1)S(1)} %collective-permute-done.3.refs_4_) | copy-start | bytes 1179652
  61.2 42.1 %collective-permute-start.5 = (bf16[1,96,2048]{2,1,0:T(8,128)(2,1)S(1)}, bf16[1,96,2048]{2,1,0:T(8,128)(2,1)S(1)}, u32[]{:S(2)}, u32[]{:S(2)}) collective-permute-start(bf16[1,96,2048]{2,1,0:T(8,128)(2,1)S(1)} %collective-permute-done.3.refs_4_), channel_id=1, source_target_pairs={{0,224},{32,0},{64,32},{96,64},{128,96},{160,128},{192,160},{224,1... | collective-permute-start | bytes 1179656 | tf_op jit(solution)/shard_map/ppermute | solution.py:343
  103.2 70.5 %copy-start.8 = (bf16[1,96,2048]{2,1,0:T(8,128)(2,1)}, bf16[1,96,2048]{2,1,0:T(8,128)(2,1)S(1)}, u32[]{:S(2)}) copy-start(bf16[1,96,2048]{2,1,0:T(8,128)(2,1)S(1)} %collective-permute-done.4.refs_5_) | copy-start | bytes 1179652
  103.2 70.5 %copy-start.9 = (bf16[1,96,2048]{2,1,0:T(8,128)(2,1)}, bf16[1,96,2048]{2,1,0:T(8,128)(2,1)S(1)}, u32[]{:S(2)}) copy-start(bf16[1,96,2048]{2,1,0:T(8,128)(2,1)S(1)} %collective-permute-done.5.refs_6_) | copy-start | bytes 1179652
  160.0 13.8 %collective-permute-start.6 = (bf16[1,96,2048]{2,1,0:T(8,128)(2,1)S(1)}, bf16[1,96,2048]{2,1,0:T(8,128)(2,1)S(1)}, u32[]{:S(2)}, u32[]{:S(2)}) collective-permute-start(bf16[1,96,2048]{2,1,0:T(8,128)(2,1)S(1)} %collective-permute-done.4.refs_5_), channel_id=1, source_target_pairs={{0,32},{32,64},{64,96},{96,128},{128,160},{160,192},{192,224},{224... | collective-permute-start | bytes 1179656 | tf_op jit(solution)/shard_map/ppermute | solution.py:343
  173.7 0.8 copy-start.10
  181.0 40.2 %all-to-all-start.2 = ((bf16[32,288,128]{2,1,0:T(8,128)(2,1)}), bf16[32,288,128]{2,1,0:T(8,128)(2,1)S(1)}, u32[]{:S(2)}, u32[]{:S(2)}) async-start(bf16[32,288,128]{2,1,0:T(8,128)(2,1)} %shard_map.59), calls=%async_computation.2 | async-start | bytes 4718592 | tf_op jit(solution)/shard_map/all_to_all | solution.py:364
  212.1 13.8 %copy-start = (bf16[512,512]{1,0:T(8,128)(2,1)S(1)}, bf16[512,512]{1,0:T(8,128)(2,1)}, u32[]{:S(2)}) copy-start(bf16[512,512]{1,0:T(8,128)(2,1)} %get-tuple-element.21.select_ref) | copy-start | bytes 1572868
  212.1 13.9 %copy-start.1 = (bf16[144,512]{1,0:T(8,128)(2,1)S(1)}, bf16[144,512]{1,0:T(8,128)(2,1)}, u32[]{:S(2)}) copy-start(bf16[144,512]{1,0:T(8,128)(2,1)} %get-tuple-element.19.mix_ref) | copy-start | bytes 442372
  212.1 13.9 %copy-start.2 = (bf16[144,64]{1,0:T(8,128)(2,1)S(1)}, bf16[144,64]{1,0:T(8,128)(2,1)}, u32[]{:S(2)}) copy-start(bf16[144,64]{1,0:T(8,128)(2,1)} %get-tuple-element.20.mix_spill_ref) | copy-start | bytes 55300
  221.2 37.9 %all-to-all-start.1 = ((bf16[32,288,128]{2,1,0:T(8,128)(2,1)}), bf16[32,288,128]{2,1,0:T(8,128)(2,1)}, u32[]{:S(2)}, u32[]{:S(2)}) async-start(bf16[32,288,128]{2,1,0:T(8,128)(2,1)} %shard_map.58), calls=%async_computation.1 | async-start | bytes 4718592 | tf_op jit(solution)/shard_map/all_to_all | solution.py:364
Sparse Core Ops, SparseCore 0:
  9.1 150.7 all-gather.2
  161.7 44.7 all-gather.4
